TPU v7x, 32 devices: a whole 2x2x4 slice. The times are simulated.
32 devices in a mesh: lat: 8 (over z, x), rad: 4 (over y, core).
Axes of the slice: x: 2, y: 2, z: 4, core: 2. Of those that a mesh axis runs over, the one named last changes fastest.
Arguments:
- kernels: float32 [3, 256000], P(None, 'lat'), may hold values from -6 to 6
- cells: int32 [3, 2048], P(None, 'lat'), may hold values from 0 to 251, as said below
- tiles: int32 [2048, 1], P('lat'), may hold values from 0 to 7; in each aligned block of 256 rows (0 to 255, 256 to 511, ...) at most 64 rows name the same one
- width_class: int32 [8], P('lat'), may hold values from 0 to 3
Outputs:
- smoothed: float32 [3, 64, 128, 256], P(None, 'lat', 'rad')
Inputs may be any that keep to these rules, and one draw needn't show every extreme that they name: `tiles`: of the elements of one index of lat, at most 64 name the same tile, a bound that some block reaches of them. cells[0, e] <= 3, cells[1, e] <= 123 and cells[2, e] <= 251, so that each element's 5 x 5 x 5 block lies in its tile; each bound is reached.
All inputs are finite; a program needn't handle non-finite values.
Results may differ from a plain program's by a relative error of at most 0.000078.
Values sent between devices are 32-bit elements; how exact they have to be, the bound alone decides.
A program may use at most 192 MiB of HBM per device.

v0:
```python
import functools

import jax
import jax.numpy as jnp
import numpy as np
from jax import lax
from jax.experimental import pallas as pl
from jax.experimental.pallas import tpu as pltpu
from jax.sharding import PartitionSpec as P

CX = 8
NY = 256
CZ = 32
NGLL = 125
HW = 4
HY = 8
HZ = 4
ZP = CZ + 4 * HZ
LANES = 128
TAPS = 2 * HZ + 1
PADX = CX + 2 * HW
PACK_UNROLL = 4
SUM_UNROLL = 4
VMEM_LIMIT = 48 * 2**20
MESH = pl.DeviceIdType.MESH


def band_matrix(count, sigma, half):
    place = np.arange(count)
    gap = place[None, :] - place[:, None]
    gauss = np.where(np.abs(gap) <= half, np.exp(-(gap**2) / (2.0 * sigma**2)), 0.0)
    return gauss / gauss.sum(axis=1, keepdims=True)


def z_taps(n_rad):
    full = np.pad(band_matrix(CZ * n_rad, 1.5, HZ), ((0, 0), (HZ, HZ)))
    return np.stack([full[z, z : z + TAPS] for z in range(CZ * n_rad)]).astype(np.float32)


def pack_kernel(
    n_lat, n_rad, share, elements, tiles_ref, cells_hbm, kern_hbm, out_ref, count, todo, place, cells_ref, kern_ref, sems
):
    slab = lax.axis_index("rad")
    rows = elements * NGLL // LANES
    bring_cells = pltpu.make_async_copy(cells_hbm, cells_ref, sems.at[0])
    bring_kern = pltpu.make_async_copy(kern_hbm, kern_ref, sems.at[1])
    bring_cells.start()
    bring_kern.start()
    out_ref[...] = jnp.full(out_ref.shape, -1000.0, jnp.float32)
    lane = lax.broadcasted_iota(jnp.int32, (3, LANES), 1)

    @pl.loop(0, n_lat)
    def _(t):
        count[t] = 0

    def listed(e, n):
        t = tiles_ref[e]
        rank = count[t]
        count[t] = rank + 1
        slot = lax.div(rank, n_rad)
        todo[n] = e
        place[n] = t * share + slot
        return n + jnp.where(rank - slot * n_rad == slab, 1, 0)

    n = lax.fori_loop(0, elements, listed, 0, unroll=4)
    for more in range(PACK_UNROLL):
        todo[n + more] = 0
        place[n + more] = n_lat * share
    bring_cells.wait()
    bring_kern.wait()

    def packed(step, _):
        for u in range(PACK_UNROLL):
            e = todo[step * PACK_UNROLL + u]
            at = place[step * PACK_UNROLL + u]
            start = e * NGLL
            row = lax.shift_right_logical(start, 7)
            off = start & (LANES - 1)
            after = jnp.minimum(row + 1, rows - 1)
            a = kern_ref[:, pl.ds(pl.multiple_of(row * LANES, LANES), LANES)]
            b = kern_ref[:, pl.ds(pl.multiple_of(after * LANES, LANES), LANES)]
            v = pltpu.roll(jnp.where(lane >= off, a, b), (LANES - off) & (LANES - 1), 1)
            v = jnp.where(lane == NGLL, cells_ref[0, e].astype(jnp.float32), v)
            v = jnp.where(lane == NGLL + 1, cells_ref[1, e].astype(jnp.float32), v)
            v = jnp.where(lane == NGLL + 2, cells_ref[2, e].astype(jnp.float32), v)
            t = lax.div(at, share)
            slot = at - t * share
            for c in range(3):
                out_ref[t, pl.ds(c * share + slot, 1), :] = v[c : c + 1]
        return 0

    lax.fori_loop(0, lax.div(n + PACK_UNROLL - 1, PACK_UNROLL), packed, 0)


def exchange_kernel(n_lat, n_rad, send_ref, recv_ref, own_sem, send_sem, recv_sem, fwd_sem, got_sem):
    tile, slab = lax.axis_index("lat"), lax.axis_index("rad")
    barrier = pltpu.get_barrier_semaphore()

    @pl.loop(1, n_lat)
    def _(k):
        pl.semaphore_signal(barrier, inc=1, device_id=(lax.rem(tile + k, n_lat), slab), device_id_type=MESH)

    pair = slab + 1 - 2 * lax.rem(slab, 2)
    other = slab + 2 - 4 * lax.div(slab, 2)
    for peer in (pair, other):
        pl.semaphore_signal(barrier, inc=1, device_id=(tile, peer), device_id_type=MESH)
    pl.semaphore_wait(barrier, n_lat - 1 + 2)

    def across(k):
        to = lax.rem(tile + k, n_lat)
        return pltpu.make_async_remote_copy(
            src_ref=send_ref.at[to],
            dst_ref=recv_ref.at[slab, tile],
            send_sem=send_sem.at[k],
            recv_sem=recv_sem.at[k],
            device_id=(to, slab),
            device_id_type=MESH,
        )

    def share(k, of, to, way):
        block = recv_ref.at[of, lax.rem(tile + n_lat - k, n_lat)]
        return pltpu.make_async_remote_copy(
            src_ref=block,
            dst_ref=block,
            send_sem=fwd_sem.at[way, k],
            recv_sem=got_sem.at[way, k],
            device_id=(tile, to),
            device_id_type=MESH,
        )

    def forward(k):
        share(k, slab, other, 0).start()
        share(k, slab, pair, 1).start()

    def relay(k):
        share(k, other, other, 0).wait_recv()
        share(k, other, pair, 2).start()

    @pl.loop(1, n_lat)
    def _(k):
        across(k).start()

    own = pltpu.make_async_copy(send_ref.at[tile], recv_ref.at[slab, tile], own_sem)
    own.start()
    own.wait()
    forward(0)

    @pl.loop(1, n_lat)
    def _(k):
        across(k).wait_recv()
        forward(k)

    @pl.loop(0, n_lat)
    def _(k):
        relay(k)

    @pl.loop(0, n_lat)
    def _(k):
        share(k, pair, pair, 1).wait_recv()
        share(k, other + pair - slab, pair, 2).wait_recv()

    @pl.loop(1, n_lat)
    def _(k):
        across(k).wait_send()

    @pl.loop(0, n_lat)
    def _(k):
        share(k, slab, other, 0).wait_send()
        share(k, slab, pair, 1).wait_send()
        share(k, other, pair, 2).wait_send()


def sum_kernel(blocks, share, meta_ref, recv_ref, acc, todo):
    slab = lax.axis_index("rad")
    slots = blocks * share
    acc[...] = jnp.zeros(acc.shape, jnp.float32)
    lane = lax.broadcasted_iota(jnp.int32, (8, LANES), 1)
    sub = lax.broadcasted_iota(jnp.int32, (8, LANES), 0)
    ramp = 25 * sub + lane
    low = slab * CZ - 2 * HZ

    def listed(s, n):
        zb = meta_ref[slots + s] - low
        todo[n] = s
        return n + jnp.where((zb >= 0) & (zb < CZ + 3 * HZ), 1, 0)

    n = lax.fori_loop(0, slots, listed, 0, unroll=8)
    for more in range(SUM_UNROLL):
        todo[n + more] = 0

    def place(at, values, index, mask):
        for j in range(5):
            picked = jnp.where(mask, index + 5 * j, NGLL)
            for c in range(3):
                piece = jnp.take_along_axis(values[c], picked, axis=1, mode="promise_in_bounds")
                acc[pl.ds(pl.multiple_of(at + (3 * j + c) * 8, 8), 8), :] += piece

    def summed(step, _):
        later = []
        for u in range(SUM_UNROLL):
            s = todo[step * SUM_UNROLL + u]
            good = step * SUM_UNROLL + u < n
            x0 = jnp.clip(meta_ref[s], 0, CX - 5)
            zb = jnp.clip(meta_ref[slots + s] - low, 0, CZ + 3 * HZ - 1)
            y0 = jnp.clip(meta_ref[2 * slots + s], 0, NY - 5)
            block = lax.div(s, share)
            slot = s - block * share
            values = []
            for c in range(3):
                row = jnp.broadcast_to(recv_ref[block, pl.ds(c * share + slot, 1), :], (8, LANES))
                values.append(jnp.where(lane < NGLL, row, 0.0))
            half = lax.shift_right_logical(y0, 7)
            yl = y0 & (LANES - 1)
            index = ramp - (25 * x0 + yl)
            rows = (sub >= x0) & (sub < jnp.where(good, x0 + 5, 0))
            at = (half * ZP + zb) * 24
            place(at, values, index, rows & (lane >= yl) & (lane < yl + 5))
            later.append((at, values, index, rows, yl))
        widest = functools.reduce(jnp.maximum, [entry[4] for entry in later])

        @pl.when(widest > LANES - 5)
        def _():
            for at, values, index, rows, yl in later:
                over = rows & (lane < yl + 5 - LANES)

                @pl.when(yl > LANES - 5)
                def _():
                    place(at + ZP * 24, values, index + LANES, over)

        return 0

    lax.fori_loop(0, lax.div(n + SUM_UNROLL - 1, SUM_UNROLL), summed, 0)


def finish_kernel(n_lat, taps_ref, wx_ref, acc, wy_ref, out_ref, planes, rows_ref, send_sem, recv_sem):
    tile, slab = lax.axis_index("lat"), lax.axis_index("rad")
    barrier = pltpu.get_barrier_semaphore()
    has_prev, has_next = tile > 0, tile < n_lat - 1
    halo = HW * CZ

    @pl.when(has_prev)
    def _():
        pl.semaphore_signal(barrier, inc=1, device_id=(tile - 1, slab), device_id_type=MESH)

    @pl.when(has_next)
    def _():
        pl.semaphore_signal(barrier, inc=1, device_id=(tile + 1, slab), device_id_type=MESH)

    def at(c, row, count):
        return rows_ref.at[:, pl.ds(c * PADX * CZ + row, count), :]

    def to_next(c):
        return pltpu.make_async_remote_copy(
            src_ref=at(c, CX * CZ, halo),
            dst_ref=at(c, 0, halo),
            send_sem=send_sem.at[0, c],
            recv_sem=recv_sem.at[0, c],
            device_id=(tile + 1, slab),
            device_id_type=MESH,
        )

    def to_prev(c):
        return pltpu.make_async_remote_copy(
            src_ref=at(c, halo, halo),
            dst_ref=at(c, halo + CX * CZ, halo),
            send_sem=send_sem.at[1, c],
            recv_sem=recv_sem.at[1, c],
            device_id=(tile - 1, slab),
            device_id_type=MESH,
        )

    for c in range(3):

        @pl.loop(0, CZ, unroll=4)
        def _(z):
            for half in range(NY // LANES):
                total = jnp.zeros((CX, LANES), jnp.float32)
                for d in range(TAPS):
                    weight = taps_ref[(slab * CZ + z) * TAPS + d]
                    row = pl.multiple_of(((half * ZP + z + HZ + d) * 3 + c) * CX, 8)
                    total = total + weight * acc[pl.ds(row, CX), :]
                cols = slice(half * LANES, (half + 1) * LANES)
                planes[pl.ds(pl.multiple_of(z * CX, 8), CX), cols] = total

        product = jnp.dot(planes[...], wy_ref[...], precision=lax.Precision.HIGHEST)
        for z in range(CZ):
            for half in range(NY // LANES):
                piece = product[z * CX : (z + 1) * CX, half * LANES : (half + 1) * LANES]
                rows_ref[half, pl.ds(c * PADX * CZ + halo + z, CX, stride=CZ), :] = piece

        if c == 0:
            beside = jnp.minimum(tile, 1) + jnp.minimum(n_lat - 1 - tile, 1)
            pl.semaphore_wait(barrier, beside)

        @pl.when(has_next)
        def _():
            to_next(c).start()

        @pl.when(has_prev)
        def _():
            to_prev(c).start()

        zeros = jnp.zeros((NY // LANES, halo, LANES), jnp.float32)

        @pl.when(tile == 0)
        def _():
            rows_ref[:, c * PADX * CZ : c * PADX * CZ + halo, :] = zeros

        @pl.when(tile == n_lat - 1)
        def _():
            rows_ref[:, c * PADX * CZ + halo + CX * CZ : (c + 1) * PADX * CZ, :] = zeros

    for c in range(3):

        @pl.when(has_prev)
        def _():
            to_next(c).wait_recv()

        @pl.when(has_next)
        def _():
            to_prev(c).wait_recv()

        @pl.loop(0, CX)
        def _(x):
            for half in range(NY // LANES):
                total = jnp.zeros((CZ, LANES), jnp.float32)
                for d in range(2 * HW + 1):
                    row = pl.multiple_of(c * PADX * CZ + (x + d) * CZ, 8)
                    total = total + wx_ref[x * (2 * HW + 1) + d] * rows_ref[half, pl.ds(row, CZ), :]
                out_ref[c, x, :, half * LANES : (half + 1) * LANES] = total

    for c in range(3):

        @pl.when(has_next)
        def _():
            to_next(c).wait_send()

        @pl.when(has_prev)
        def _():
            to_prev(c).wait_send()


def x_weights(width_class, n_lat):
    rows = lax.axis_index("lat") * CX + jnp.arange(CX)
    sigma = 1.0 + 0.75 * width_class[0].astype(jnp.float32)
    offsets = jnp.arange(-HW, HW + 1)
    target = rows[:, None] + offsets[None, :]
    valid = (target >= 0) & (target < CX * n_lat)
    gauss = jnp.exp(-(offsets[None, :].astype(jnp.float32) ** 2) / (2.0 * sigma**2))
    gauss = jnp.where(valid, gauss, 0.0)
    return gauss / jnp.sum(gauss, axis=1, keepdims=True)


def on_device(n_lat, n_rad, kernels, cells, tiles, width_class):
    elements = tiles.shape[0]
    cap = max(2, 2 * elements // n_lat)
    share = -(-cap // n_rad)
    blocks = n_rad * n_lat
    slots = blocks * share
    params = pltpu.CompilerParams(vmem_limit_bytes=VMEM_LIMIT)
    smem = pl.BlockSpec(memory_space=pltpu.SMEM)
    vmem = pl.BlockSpec(memory_space=pltpu.VMEM)
    hbm = pl.BlockSpec(memory_space=pl.ANY)
    send = pl.pallas_call(
        functools.partial(pack_kernel, n_lat, n_rad, share, elements),
        out_shape=jax.ShapeDtypeStruct((n_lat + 1, 3 * share, LANES), jnp.float32),
        in_specs=[smem, hbm, hbm],
        out_specs=vmem,
        scratch_shapes=[
            pltpu.SMEM((n_lat,), jnp.int32),
            pltpu.SMEM((elements + PACK_UNROLL,), jnp.int32),
            pltpu.SMEM((elements + PACK_UNROLL,), jnp.int32),
            pltpu.SMEM(cells.shape, jnp.int32),
            pltpu.VMEM(kernels.shape, jnp.float32),
            pltpu.SemaphoreType.DMA((2,)),
        ],
        compiler_params=params,
    )(tiles.reshape(-1), cells, kernels)
    recv = pl.pallas_call(
        functools.partial(exchange_kernel, n_lat, n_rad),
        out_shape=jax.ShapeDtypeStruct((n_rad, n_lat, 3 * share, LANES), jnp.float32),
        in_specs=[vmem],
        out_specs=vmem,
        scratch_shapes=[
            pltpu.SemaphoreType.DMA,
            pltpu.SemaphoreType.DMA((n_lat,)),
            pltpu.SemaphoreType.DMA((n_lat,)),
            pltpu.SemaphoreType.DMA((3, n_lat)),
            pltpu.SemaphoreType.DMA((3, n_lat)),
        ],
        compiler_params=pltpu.CompilerParams(
            vmem_limit_bytes=VMEM_LIMIT, collective_id=0, has_side_effects=True
        ),
    )(send)
    recv = recv.reshape(blocks, 3 * share, LANES)
    meta = recv[:, :share, NGLL:].transpose(2, 0, 1).reshape(-1).astype(jnp.int32)
    grid_rows = NY // LANES * ZP * 24
    summed = pl.pallas_call(
        functools.partial(sum_kernel, blocks, share),
        out_shape=jax.ShapeDtypeStruct((grid_rows, LANES), jnp.float32),
        in_specs=[smem, vmem],
        out_specs=vmem,
        scratch_shapes=[pltpu.SMEM((slots + SUM_UNROLL,), jnp.int32)],
        compiler_params=params,
    )(meta, recv)
    return pl.pallas_call(
        functools.partial(finish_kernel, n_lat),
        out_shape=jax.ShapeDtypeStruct((3, CX, CZ, NY), jnp.float32),
        in_specs=[smem, smem, vmem, vmem],
        out_specs=vmem,
        scratch_shapes=[
            pltpu.VMEM((CZ * CX, NY), jnp.float32),
            pltpu.VMEM((NY // LANES, 3 * PADX * CZ, LANES), jnp.float32),
            pltpu.SemaphoreType.DMA((2, 3)),
            pltpu.SemaphoreType.DMA((2, 3)),
        ],
        compiler_params=pltpu.CompilerParams(
            vmem_limit_bytes=VMEM_LIMIT, collective_id=1, has_side_effects=True
        ),
    )(
        jnp.asarray(z_taps(n_rad).reshape(-1)),
        x_weights(width_class, n_lat).reshape(-1),
        summed,
        jnp.asarray(band_matrix(NY, 2.5, HY).T.astype(np.float32)),
    )


def solution(mesh):
    return jax.shard_map(
        functools.partial(on_device, mesh.shape["lat"], mesh.shape["rad"]),
        mesh=mesh,
        in_specs=(P(None, "lat"), P(None, "lat"), P("lat", None), P("lat")),
        out_specs=P(None, "lat", "rad", None),
        check_vma=False,
    )
```

profile of v0, /device:TPU:25, one launch (start us, length us, event | category | flops | bytes accessed | tf_op | source)
XLA Modules:
  0.0 55.1 jit_solution(16753007341800574049)
XLA Ops:
  0.7 0.2 select_reduce_fusion
  0.9 0.1 select_divide_fusion
  1.0 0.1 reshape.52.wx_ref
  1.0 0.0 copy-start
  1.0 1.0 %copy-done = f32[3,32000]{1,0:T(4,128)S(1)} copy-done((f32[3,32000]{1,0:T(4,128)S(1)}, f32[3,32000]{1,0:T(4,128)}, u32[]{:S(2)}) %copy-start) | copy-done | bytes 384024
  2.1 0.0 copy-start.3
  2.1 0.7 %copy-done.3 = s32[3,256]{1,0:T(4,128)S(1)} copy-done((s32[3,256]{1,0:T(4,128)S(1)}, s32[3,256]{1,0:T(4,128)}, u32[]{:S(2)}) %copy-start.3) | copy-done | bytes 3096
  2.8 0.0 copy-start.4
  2.8 0.7 %copy-done.4 = s32[256,1]{0,1:T(1,128)S(1)} copy-done((s32[256,1]{0,1:T(1,128)S(1)}, s32[256,1]{0,1:T(1,128)}, u32[]{:S(2)}) %copy-start.4) | copy-done | bytes 1048
  3.5 4.4 %shard_map.64.send_ref = f32[9,48,128]{2,1,0:T(8,128)S(1)} custom-call(s32[256]{0:T(256)S(1)} %bitcast.7, s32[3,256]{1,0:T(4,128)S(1)} %copy-done.3, f32[3,32000]{1,0:T(4,128)S(1)} %copy-done), custom_call_target="tpu_custom_call" | custom-call | tf_op jit(solution)/shard_map/pallas_call | solution.py:364
  7.9 14.7 %shard_map.65 = f32[4,8,48,128]{3,2,1,0:T(8,128)S(1)} custom-call(f32[9,48,128]{2,1,0:T(8,128)S(1)} %shard_map.64.send_ref), custom_call_target="tpu_custom_call" | custom-call | tf_op jit(solution)/shard_map/pallas_call | solution.py:379
  22.6 0.1 fusion
  22.7 0.0 copy-start.1
  22.7 0.0 copy-start.2
  22.7 0.3 copy.7
  23.0 0.1 convert_element_type.23.meta_ref
  23.1 12.2 %shard_map.66.acc = f32[2304,128]{1,0:T(8,128)S(1)} custom-call(s32[1536]{0:T(1024)S(1)} %convert_element_type.23.meta_ref, f32[32,48,128]{2,1,0:T(8,128)S(1)} %bitcast.6), custom_call_target="tpu_custom_call" | custom-call | tf_op jit(solution)/shard_map/pallas_call | solution.py:398
  35.4 0.0 copy-done.1
  35.4 0.0 copy-done.2
  35.4 18.8 %shard_map.67 = f32[3,8,32,256]{3,2,1,0:T(8,128)S(1)} custom-call(f32[1152]{0:T(1024)S(1)} %copy-done.2, f32[72]{0:T(128)S(1)} %reshape.52.wx_ref, f32[2304,128]{1,0:T(8,128)S(1)} %shard_map.66.acc, f32[256,256]{1,0:T(8,128)S(1)} %copy-done.1), custom_call_target="tpu_custom_call" | custom-call | tf_op jit(solution)/shard_map/pallas_call | solution.py:406
  54.2 0.9 %copy.10 = f32[3,8,32,256]{3,2,1,0:T(8,128)} copy(f32[3,8,32,256]{3,2,1,0:T(8,128)S(1)} %shard_map.67) | data formatting | bytes 1572864
  (3 shorter events, 0.0 us)
Async XLA Ops:
  1.0 1.0 %copy-start = (f32[3,32000]{1,0:T(4,128)S(1)}, f32[3,32000]{1,0:T(4,128)}, u32[]{:S(2)}) copy-start(f32[3,32000]{1,0:T(4,128)} %kern_hbm.1) | copy-start | bytes 1152004
  2.1 0.7 %copy-start.3 = (s32[3,256]{1,0:T(4,128)S(1)}, s32[3,256]{1,0:T(4,128)}, u32[]{:S(2)}) copy-start(s32[3,256]{1,0:T(4,128)} %cells_hbm.1) | copy-start | bytes 9220
  2.8 0.7 %copy-start.4 = (s32[256,1]{0,1:T(1,128)S(1)}, s32[256,1]{0,1:T(1,128)}, u32[]{:S(2)}) copy-start(s32[256,1]{0,1:T(1,128)} %param.8) | copy-start | bytes 3076
  22.7 12.6 %copy-start.1 = (f32[256,256]{1,0:T(8,128)S(1)}, f32[256,256]{1,0:T(8,128)}, u32[]{:S(2)}) copy-start(f32[256,256]{1,0:T(8,128)} %constant.29.clone.wy_ref) | copy-start | bytes 786436
  22.7 12.6 %copy-start.2 = (f32[1152]{0:T(1024)S(1)}, f32[1152]{0:T(1024)}, u32[]{:S(2)}) copy-start(f32[1152]{0:T(1024)} %constant.28.clone.taps_ref) | copy-start | bytes 13828
where the time goes:
time: 55.3 us; the launch traced here: 55.1 us
  Pallas kernels  50.2 us (91%)
  local copies, waits for them, and re-layouts  3.74 us (7%)
  between operations  0.75 us (1%)
    pallas_call x1, Pallas kernels, on_device(): pl.pallas_call(functools.partial(finish_kernel, n_lat), out_shape=jax.Sha...  18.8 us
    pallas_call x1, Pallas kernels, on_device(): pl.pallas_call(functools.partial(exchange_kernel, n_lat, n_rad), out_shap...  14.7 us
    pallas_call x1, Pallas kernels, on_device(): pl.pallas_call(functools.partial(sum_kernel, blocks, share), out_shape=ja...  12.2 us
    pallas_call x1, Pallas kernels, on_device(): pl.pallas_call(functools.partial(pack_kernel, n_lat, n_rad, share, elemen...  4.45 us
    unnamed x11, local copies, waits for them, and re-layouts  3.3 us

commit v1 on v0

--- a/solution.py
+++ b/solution.py
@@ -424,10 +424,455 @@
         jnp.asarray(band_matrix(NY, 2.5, HY).T.astype(np.float32)),
     )
 
+ROW_TILES = 3
+Z_BINS = 11
+Y_TILES = 17
+WINDOW = CZ + 2 * HZ
+DEPTH = 2 * CX * WINDOW
+SUM_WAYS = 4
+
+
+def gather_kernel(n_lat, n_rad, block, width_ref, tiles_hbm, cells_hbm, kern_hbm, data_ref, words_ref, whi_ref, wlo_ref,
+                  kern_ref, tiles_ref, cells_ref, index_ref, compact_ref, in_sem, is_sem, ir_sem, zs, zr, xs, xr, ys, yr, bs, br):
+    lat, rad = lax.axis_index("lat"), lax.axis_index("rad")
+    levels = n_lat // 2
+    z, x = lax.div(lat, 2), lax.rem(lat, 2)
+    y, k = lax.div(rad, 2), lax.rem(rad, 2)
+    across_x, across_y, across_k = lat + 1 - 2 * x, rad + 2 - 4 * y, rad + 1 - 2 * k
+    barrier = pltpu.get_barrier_semaphore()
+
+    @pl.loop(1, n_lat)
+    def _(step):
+        pl.semaphore_signal(barrier, inc=1, device_id=(lax.rem(lat + step, n_lat), rad), device_id_type=MESH)
+
+    for peer in (across_y, across_k):
+        pl.semaphore_signal(barrier, inc=1, device_id=(lat, peer), device_id_type=MESH)
+    brought = [
+        pltpu.make_async_copy(kern_hbm, kern_ref, in_sem.at[0]),
+        pltpu.make_async_copy(tiles_hbm, tiles_ref, in_sem.at[1]),
+        pltpu.make_async_copy(cells_hbm, cells_ref, in_sem.at[2]),
+    ]
+    for copy in brought:
+        copy.start()
+
+    half = block // 2
+    edge = half // 8 // 3 * 8 + 8
+    inner = half - 2 * edge
+    mine = k * half
+    spans = {"send": (mine + y * (edge + inner), edge), "inner": (mine + edge, inner), "take": (mine + (1 - y) * (edge + inner), edge)}
+    theirs = (1 - k) * half
+    other = {"send": (theirs + y * (edge + inner), edge), "inner": (theirs + edge, inner), "take": (theirs + (1 - y) * (edge + inner), edge)}
+    parts = ("send", "inner")
+
+    def piece(i, span):
+        return data_ref.at[pl.ds(pl.multiple_of(i * block + span[0], 8), span[1])]
+
+    def move(i, span, send_sem, recv_sem, device):
+        return pltpu.make_async_remote_copy(
+            src_ref=piece(i, span), dst_ref=piece(i, span), send_sem=send_sem, recv_sem=recv_sem,
+            device_id=device, device_id_type=MESH)
+
+    def z_move(i, j, up):
+        return move(i, spans[parts[j]], zs.at[i, 2 * j + (0 if up else 1)], zr.at[i, j], (lat + (2 if up else -2), rad))
+
+    def x_move(i, j):
+        return move(i, spans[parts[j]], xs.at[i, j], xr.at[i, j], (across_x, rad))
+
+    def y_move(i, name):
+        return move(i, spans[name], ys.at[i], yr.at[i], (lat, across_y))
+
+    def k_move(i, j, of):
+        return move(i, of[("send", "inner", "take")[j]], bs.at[i, j], br.at[i, j], (lat, across_k))
+
+    def index_move(step):
+        to = lax.rem(lat + step, n_lat)
+        return pltpu.make_async_remote_copy(
+            src_ref=index_ref.at[lat], dst_ref=index_ref.at[lat], send_sem=is_sem.at[step], recv_sem=ir_sem.at[step],
+            device_id=(to, rad), device_id_type=MESH)
+
+    def index_take(step):
+        whose = index_ref.at[lax.rem(lat + n_lat - step, n_lat)]
+        return pltpu.make_async_remote_copy(
+            src_ref=whose, dst_ref=whose, send_sem=is_sem.at[step], recv_sem=ir_sem.at[step],
+            device_id=(lax.rem(lat + step, n_lat), rad), device_id_type=MESH)
+
+    can_up, can_down = z < levels - 1, z > 0
+    brought[1].wait()
+    brought[2].wait()
+    index_ref[lat] = jnp.concatenate([tiles_ref[...], cells_ref[...], jnp.zeros((4, tiles_ref.shape[1]), jnp.int32)], axis=0)
+    brought[0].wait()
+    base = pl.multiple_of(lat * block, 8)
+    lane_tiles = kern_ref.shape[1] // LANES
+    groups = lane_tiles // 8
+
+    def packed(at, row, count):
+        rows = [kern_ref[:, pl.ds(pl.multiple_of(at + u * LANES, LANES), LANES)] for u in range(count)]
+        return jnp.concatenate(rows, axis=0)
+
+    @pl.loop(0, groups, unroll=4)
+    def _(g):
+        data_ref[pl.ds(base + pl.multiple_of(g * 24, 8), 24), :] = packed(g * 8 * LANES, 0, 8)
+
+    left = lane_tiles - groups * 8
+    if left:
+        tail = packed(groups * 8 * LANES, 0, left)
+        room = block - groups * 24
+        tail = jnp.concatenate([tail, jnp.zeros((room - 3 * left, LANES), jnp.float32)], axis=0)
+        data_ref[pl.ds(base + groups * 24, room), :] = tail
+    pl.semaphore_wait(barrier, n_lat - 1 + 2)
+
+    @pl.loop(1, n_lat)
+    def _(step):
+        index_move(step).start()
+
+    for j in range(2):
+        @pl.when(can_up)
+        def _():
+            z_move(lat, j, True).start()
+
+        @pl.when(can_down)
+        def _():
+            z_move(lat, j, False).start()
+
+        x_move(lat, j).start()
+
+    def weights():
+        col = lax.broadcasted_iota(jnp.int32, (8, DEPTH), 1)
+        beside = col >= CX * WINDOW
+        rest = jnp.where(beside, col - CX * WINDOW, col)
+        xl = lax.shift_right_logical(rest * 1639, 16)
+        zc = rest - WINDOW * xl
+        place = jnp.where(beside, jnp.where(xl < HW, xl + CX, xl - CX), xl)
+        sub = lax.broadcasted_iota(jnp.int32, (8, DEPTH), 0)
+        sigma = 1.0 + 0.75 * jnp.full((8, DEPTH), width_ref[0], jnp.int32).astype(jnp.float32)
+        twice = 2.0 * sigma * sigma
+
+        def bell(d, reach, scale):
+            square = (d * d).astype(jnp.float32)
+            return jnp.where(jnp.abs(d) <= reach, jnp.exp(-square / scale), 0.0)
+
+        norm = jnp.zeros((8, DEPTH), jnp.float32)
+        for d in range(-HW, HW + 1):
+            at = lat * CX + sub + d
+            norm += jnp.where((at >= 0) & (at < CX * n_lat), jnp.exp(-float(d * d) / twice), 0.0)
+        wx = bell(place - sub, HW, twice) / norm
+        for zv in range(CZ // 8):
+            norm = jnp.zeros((8, DEPTH), jnp.float32)
+            zz = sub + 8 * zv
+            for d in range(-HZ, HZ + 1):
+                at = rad * CZ + zz + d
+                norm += jnp.where((at >= 0) & (at < CZ * n_rad), float(np.exp(-d * d / 4.5)), 0.0)
+            kern_w[zv * 8 : zv * 8 + 8, :] = bell(zc - HZ - zz, HZ, 4.5) / norm
+        for xx in range(CX):
+            both = kern_w[...] * wx[xx : xx + 1, :]
+            high = both.astype(jnp.bfloat16)
+            whi_ref[xx * CZ : xx * CZ + CZ, :] = high
+            wlo_ref[xx * CZ : xx * CZ + CZ, :] = (both - high.astype(jnp.float32)).astype(jnp.bfloat16)
+
+    kern_w = compact_ref.at[pl.ds(0, CZ)]
+    weights()
+
+    def lists():
+        @pl.loop(1, n_lat)
+        def _(step):
+            index_take(step).wait_recv()
+
+        elements = index_ref.shape[2]
+        shape = (n_lat, elements)
+        rel = index_ref[:, 0, :] - lat
+        x0 = index_ref[:, 1, :]
+        zq = index_ref[:, 2, :] - rad * CZ + HZ + 8
+        y0 = index_ref[:, 3, :]
+        keep = (rel >= -1) & (rel <= 1) & (zq >= 4) & (zq < WINDOW + 8)
+        before = lax.broadcasted_iota(jnp.int32, (elements, elements), 0) < lax.broadcasted_iota(jnp.int32, (elements, elements), 1)
+        flags = jnp.where(keep, 1.0, 0.0)
+        rank = jnp.dot(flags.astype(jnp.bfloat16), jnp.where(before, 1.0, 0.0).astype(jnp.bfloat16), preferred_element_type=jnp.float32)
+        total = jnp.sum(flags, axis=1, keepdims=True).astype(jnp.int32)
+        rank = jnp.where(keep, rank, -1.0)
+        low = jnp.maximum(x0, jnp.where(rel < 0, HW, 0))
+        high = jnp.minimum(x0 + 4, jnp.where(rel > 0, HW - 1, CX - 1))
+        code = low + 8 * (high - low + 1)
+        lane = lax.broadcasted_iota(jnp.int32, shape, 1)
+        fields = [lane, zq, y0, x0, code, jnp.where(rel == 0, 0, 1)]
+        fields = [jnp.where(keep, f, 0).astype(jnp.float32) for f in fields]
+        slot = lax.broadcasted_iota(jnp.int32, (elements, elements), 0).astype(jnp.float32)
+        zero = jnp.zeros((1, elements), jnp.float32)
+        for i in range(n_lat):
+            stack = jnp.concatenate([f[i : i + 1] for f in fields] + [zero, zero], axis=0).astype(jnp.bfloat16)
+            pick = jnp.where(rank[i : i + 1] == slot, 1.0, 0.0).astype(jnp.bfloat16)
+            compact_ref[8 * i : 8 * i + 8, :elements] = lax.dot_general(
+                stack, pick, (((1,), (1,)), ((), ())), preferred_element_type=jnp.float32)
+
+        def field(f):
+            return jnp.concatenate([compact_ref[8 * i + f : 8 * i + f + 1, :elements] for i in range(n_lat)], axis=0).astype(jnp.int32)
+
+        e, zq, y0, x0, code, beside = [field(f) for f in range(6)]
+        start = e * NGLL
+        row = lax.broadcasted_iota(jnp.int32, shape, 0) * block + 3 * lax.shift_right_logical(start, 7)
+        off = start & (LANES - 1)
+        words = row | (off << 16) | (((off - 25 * x0) & (LANES - 1)) << 23)
+        words_ref[0] = jnp.where(lane == elements - 1, total, words)
+        zb = jnp.maximum(lax.shift_right_logical(zq, 2) - 1, 0)
+        at = ((beside * Z_BINS + zb) * Y_TILES + lax.shift_right_logical(y0, 4)) * 8
+        words_ref[1] = at | ((zq & 7) << 16) | ((y0 & 15) << 20) | (code << 24)
+
+    def when_there(d, up, body):
+        zi = z - d if up else z + d
+
+        @pl.when((zi >= 0) & (zi < levels))
+        def _():
+            body(2 * zi)
+
+    def line(d, up, j):
+        def body(i):
+            i = i + x
+            z_move(i, j, up).wait_recv()
+
+            @pl.when(can_up if up else can_down)
+            def _():
+                z_move(i, j, up).start()
+
+            x_move(i, j).start()
+            if j == 0:
+                y_move(i, "send").start()
+            k_move(i, j, spans).start()
+
+        when_there(d, up, body)
+
+    def cross(d, up, j):
+        def body(i):
+            i = i + 1 - x
+            x_move(i, j).wait_recv()
+            if j == 0:
+                y_move(i, "send").start()
+            k_move(i, j, spans).start()
+
+        when_there(d, up, body)
+
+    def y_done(d, up, column):
+        def body(i):
+            i = i + column
+            y_move(i, "take").wait_recv()
+            k_move(i, 2, spans).start()
+
+        when_there(d, up, body)
+
+    ways = lambda d: (True, False) if d else (True,)
+    for d in range(1, levels + 2):
+        for j in range(2):
+            if d < levels:
+                for up in ways(d):
+                    line(d, up, j)
+            if d - 1 < levels:
+                for up in ways(d - 1):
+                    cross(d - 1, up, j)
+            if j == 0 and d == 1:
+                lists()
+            if j == 0 and 1 <= d - 1 < levels:
+                for up in ways(d - 1):
+                    y_done(d - 1, up, x)
+            if j == 0 and 0 <= d - 2 < levels:
+                for up in ways(d - 2):
+                    y_done(d - 2, up, 1 - x)
+
+    @pl.loop(1, n_lat)
+    def _(step):
+        index_move(step).wait_send()
+
+    @pl.loop(0, n_lat)
+    def _(i):
+        @pl.when(i != lat)
+        def _():
+            for j in range(3):
+                k_move(i, j, other).wait_recv()
+                k_move(i, j, spans).wait_send()
+            y_move(i, "send").wait_send()
+
+    @pl.loop(0, levels)
+    def _(zi):
+        i = 2 * zi + x
+        for j in range(2):
+            x_move(i, j).wait_send()
+
+            @pl.when(can_up & (zi <= z))
+            def _():
+                z_move(i, j, True).wait_send()
+
+            @pl.when(can_down & (zi >= z))
+            def _():
+                z_move(i, j, False).wait_send()
+
+
+def grid_kernel(n_lat, words_ref, data_ref, whi_ref, wlo_ref, ghi_hbm, glo_hbm, out_hbm, acc0, acc1, acc2, field, result, words, ghi_ref, glo_ref, sem, smooth_sem, out_sem):
+    accs = (acc0, acc1, acc2)
+    smooth = [pltpu.make_async_copy(ghi_hbm, ghi_ref, smooth_sem.at[0]), pltpu.make_async_copy(glo_hbm, glo_ref, smooth_sem.at[1])]
+    bring = pltpu.make_async_copy(words_ref, words, sem)
+    bring.start()
+    for copy in smooth:
+        copy.start()
+    rows = acc0.shape[0]
+
+    @pl.loop(0, rows // 8, unroll=11)
+    def _(r):
+        for acc in accs:
+            acc[pl.ds(pl.multiple_of(r * 8, 8), 8), :] = jnp.zeros((8, LANES), jnp.float32)
+
+    bring.wait()
+    lane = lax.broadcasted_iota(jnp.int32, (8, LANES), 1)
+    sub = lax.broadcasted_iota(jnp.int32, (8, LANES), 0)
+    across = lane & 15
+    along = lax.shift_right_logical(lane, 4)
+    ramp = 25 * along
+    elements = words.shape[2]
+
+    @pl.loop(0, n_lat)
+    def _(i):
+        count = words[0, i, elements - 1]
+
+        @pl.loop(0, lax.div(count + SUM_WAYS - 1, SUM_WAYS))
+        def _(step):
+            for u in range(SUM_WAYS):
+                p = step * SUM_WAYS + u
+                w0, w1 = words[0, i, p], words[1, i, p]
+                row = w0 & 0xFFFF
+                off = lax.shift_right_logical(w0, 16) & 127
+                shift = lax.shift_right_logical(w0, 23)
+                at = pl.multiple_of(w1 & 0xFFFF, 8)
+                zq = lax.shift_right_logical(w1, 16) & 7
+                yl = lax.shift_right_logical(w1, 20) & 15
+                low = lax.shift_right_logical(w1, 24) & 7
+                wide = lax.shift_right_logical(w1, 27)
+                tz = (sub - zq) & 7
+                ty = (lane - yl) & 15
+                tx = along - low
+                index = (ramp + shift + 5 * tz + ty) & (LANES - 1)
+                good = (tz < 5) & (ty < 5) & (tx >= 0) & (tx < wide)
+                first = across >= yl
+                here, there = good & first, good & jnp.logical_not(first)
+                head = lane >= off
+                for c in range(3):
+                    a = jnp.broadcast_to(data_ref[pl.ds(row + c, 1), :], (8, LANES))
+                    b = jnp.broadcast_to(data_ref[pl.ds(row + 3 + c, 1), :], (8, LANES))
+                    v = jnp.take_along_axis(jnp.where(head, a, b), index, axis=1, mode="promise_in_bounds")
+                    accs[c][pl.ds(at, 8), :] += jnp.where(here, v, 0.0)
+                    accs[c][pl.ds(at + 8, 8), :] += jnp.where(there, v, 0.0)
+
+    low_half = sub < 4
+    for copy in smooth:
+        copy.wait()
+    for c in range(3):
+        acc = accs[c]
+
+        @pl.loop(0, 2)
+        def _(g):
+            @pl.loop(0, WINDOW // 8)
+            def _(h):
+                for side in range(2):
+                    v = []
+                    for t in range(8):
+                        def bins(n):
+                            r = ((g * Z_BINS + 2 * h + n) * Y_TILES + side * 8 + t) * 8
+                            return acc[pl.ds(pl.multiple_of(r, 8), 8), :]
+
+                        v.append(bins(1) + jnp.where(low_half, bins(0), bins(2)))
+                    for bit in (4, 2, 1):
+                        straight = (along & bit) == 0
+                        w = list(v)
+                        for r in range(8):
+                            if r & bit:
+                                continue
+                            a, b = v[r], v[r + bit]
+                            if bit == 4:
+                                turned = pltpu.roll(jnp.where(straight, b, a), 64, 1)
+                                w[r] = jnp.where(straight, a, turned)
+                                w[r + bit] = jnp.where(straight, turned, b)
+                            else:
+                                w[r] = jnp.where(straight, a, pltpu.roll(b, 16 * bit, 1))
+                                w[r + bit] = jnp.where(straight, pltpu.roll(a, LANES - 16 * bit, 1), b)
+                        v = w
+                    for xl in range(8):
+                        r = pl.multiple_of(g * (CX * WINDOW) + xl * WINDOW + h * 8, 8)
+                        field[pl.ds(r, 8), side * LANES : (side + 1) * LANES] = v[xl]
+
+        def split(a):
+            high = a.astype(jnp.bfloat16)
+            return high, (a - high.astype(jnp.float32)).astype(jnp.bfloat16)
+
+        def dot(a, b):
+            return jnp.dot(a, b, preferred_element_type=jnp.float32)
+
+        high, low = split(field[...])
+        whi = whi_ref[...]
+        mixed = dot(whi, high) + dot(wlo_ref[...], high) + dot(whi, low)
+        high, low = split(mixed)
+        ghi = ghi_ref[...]
+        done = dot(high, ghi) + dot(low, ghi) + dot(high, glo_ref[...])
+        result[c] = done.reshape(CX, CZ, NY)
+        pltpu.make_async_copy(result.at[c], out_hbm.at[c], out_sem.at[c]).start()
+    for c in range(3):
+        pltpu.make_async_copy(result.at[c], out_hbm.at[c], out_sem.at[c]).wait()
+
+
+def on_device_whole(n_lat, n_rad, kernels, cells, tiles, width_class):
+    elements = tiles.shape[0]
+    block = -(-kernels.shape[1] // LANES * 3 // 16) * 16
+    smem = pl.BlockSpec(memory_space=pltpu.SMEM)
+    vmem = pl.BlockSpec(memory_space=pltpu.VMEM)
+    hbm = pl.BlockSpec(memory_space=pltpu.HBM)
+    dma = pltpu.SemaphoreType.DMA
+    data, words, whi, wlo = pl.pallas_call(
+        functools.partial(gather_kernel, n_lat, n_rad, block),
+        out_shape=[
+            jax.ShapeDtypeStruct((n_lat * block + 8, LANES), jnp.float32),
+            jax.ShapeDtypeStruct((2, n_lat, elements), jnp.int32),
+            jax.ShapeDtypeStruct((CX * CZ, DEPTH), jnp.bfloat16),
+            jax.ShapeDtypeStruct((CX * CZ, DEPTH), jnp.bfloat16),
+        ],
+        in_specs=[smem, hbm, hbm, hbm],
+        out_specs=[vmem] * 4,
+        scratch_shapes=[
+            pltpu.VMEM(kernels.shape, jnp.float32),
+            pltpu.VMEM((1, elements), jnp.int32),
+            pltpu.VMEM(cells.shape, jnp.int32),
+            pltpu.VMEM((n_lat, 8, elements), jnp.int32),
+            pltpu.VMEM((8 * n_lat, DEPTH), jnp.float32),
+            dma((3,)), dma((n_lat,)), dma((n_lat,)),
+            dma((n_lat, 4)), dma((n_lat, 2)), dma((n_lat, 2)), dma((n_lat, 2)),
+            dma((n_lat,)), dma((n_lat,)), dma((n_lat, 3)), dma((n_lat, 3)),
+        ],
+        compiler_params=pltpu.CompilerParams(
+            vmem_limit_bytes=VMEM_LIMIT, collective_id=0, has_side_effects=True
+        ),
+    )(width_class, tiles.reshape(1, elements), cells, kernels)
+    smooth = band_matrix(NY, 2.5, HY).T.astype(np.float32)
+    high = smooth.astype(jnp.bfloat16)
+    low = (smooth - high.astype(np.float32)).astype(jnp.bfloat16)
+    rows = 2 * Z_BINS * Y_TILES * 8
+    return pl.pallas_call(
+        functools.partial(grid_kernel, n_lat),
+        out_shape=jax.ShapeDtypeStruct((3, CX, CZ, NY), jnp.float32),
+        in_specs=[vmem] * 4 + [hbm] * 2,
+        out_specs=hbm,
+        scratch_shapes=[
+            pltpu.VMEM((rows, LANES), jnp.float32),
+            pltpu.VMEM((rows, LANES), jnp.float32),
+            pltpu.VMEM((rows, LANES), jnp.float32),
+            pltpu.VMEM((DEPTH, NY), jnp.float32),
+            pltpu.VMEM((3, CX, CZ, NY), jnp.float32),
+            pltpu.SMEM((2, n_lat, elements), jnp.int32),
+            pltpu.VMEM((NY, NY), jnp.bfloat16),
+            pltpu.VMEM((NY, NY), jnp.bfloat16),
+            dma, dma((2,)), dma((3,)),
+        ],
+        compiler_params=pltpu.CompilerParams(vmem_limit_bytes=VMEM_LIMIT),
+    )(words, data, whi, wlo, jnp.asarray(high), jnp.asarray(low))
+
 
 def solution(mesh):
+    n_lat, n_rad = mesh.shape["lat"], mesh.shape["rad"]
+    whole = n_lat <= 8 and n_lat % 2 == 0 and n_rad == 4
     return jax.shard_map(
-        functools.partial(on_device, mesh.shape["lat"], mesh.shape["rad"]),
+        functools.partial(on_device_whole if whole else on_device, n_lat, n_rad),
         mesh=mesh,
         in_specs=(P(None, "lat"), P(None, "lat"), P("lat", None), P("lat")),
         out_specs=P(None, "lat", "rad", None),

time: 55.3 us -> 50.1 us (0.906); the launches traced: 55.1 us -> 50.7 us
  Pallas kernels: 50.2 us -> 45.8 us
    pallas_call x4 -> x2, Pallas kernels: 50.2 us -> 45.8 us  [the longest x1 23.5 us: on_device_whole(): pl.pallas_call(functools.partial(gather_kernel, n_lat, n_rad, block), out...]
    unnamed x11 -> x10, local copies, waits for them, and re-layouts: 3.3 us -> 4.2 us
where the time goes in v1:
time: 50.1 us; the launch traced here: 50.7 us
  Pallas kernels  45.8 us (91%)
  local copies, waits for them, and re-layouts  4.2 us (8%)
  between operations  0.68 us (1%)
    pallas_call x1, Pallas kernels, on_device_whole(): pl.pallas_call(functools.partial(gather_kernel, n_lat, n_rad, block), out...  23.5 us
    pallas_call x1, Pallas kernels, on_device_whole(): pl.pallas_call(functools.partial(grid_kernel, n_lat), out_shape=jax.Shape...  22.3 us
    unnamed x10, local copies, waits for them, and re-layouts  4.2 us

profile of v1, /device:TPU:25, one launch (start us, length us, event | category | flops | bytes accessed | tf_op | source)
XLA Modules:
  0.0 50.7 jit_solution(10443208525997109118)
XLA Ops:
  0.7 0.0 copy-start
  0.7 1.0 %copy-done = f32[3,32000]{1,0:T(4,128)S(1)} copy-done((f32[3,32000]{1,0:T(4,128)S(1)}, f32[3,32000]{1,0:T(4,128)}, u32[]{:S(2)}) %copy-start) | copy-done | bytes 384024
  1.7 0.0 copy-start.3
  1.7 0.7 %copy-done.3 = s32[3,256]{1,0:T(4,128)S(1)} copy-done((s32[3,256]{1,0:T(4,128)S(1)}, s32[3,256]{1,0:T(4,128)}, u32[]{:S(2)}) %copy-start.3) | copy-done | bytes 3096
  2.4 0.0 copy-start.4
  2.4 0.7 %copy-done.4 = s32[256,1]{0,1:T(1,128)S(1)} copy-done((s32[256,1]{0,1:T(1,128)S(1)}, s32[256,1]{0,1:T(1,128)}, u32[]{:S(2)}) %copy-start.4) | copy-done | bytes 1048
  3.1 23.5 %shard_map.64 = (f32[6024,128]{1,0:T(8,128)S(1)}, s32[2,8,256]{2,1,0:T(8,128)S(1)}, bf16[256,640]{1,0:T(8,128)(2,1)S(1)}, bf16[256,640]{1,0:T(8,128)(2,1)S(1)}) custom-call(s32[1]{0:T(128)S(6)} %copy.7.width_ref, s32[1,256]{1,0:T(1,128)S(1)} %bitcast.1, s32[3,256]{1,0:T(4,128)S(1)} %copy-done.3, f32[3,32000]{1,0:T(4,128)S(1)} %copy-done), custom_call_target="tpu_custom_call" | custom-call | tf_op jit(solution)/shard_map/pallas_call | solution.py:823
  26.5 0.0 copy-start.1
  26.6 0.9 %copy-done.1 = bf16[256,256]{1,0:T(8,128)(2,1)S(1)} copy-done((bf16[256,256]{1,0:T(8,128)(2,1)S(1)}, bf16[256,256]{1,0:T(8,128)(2,1)}, u32[]{:S(2)}) %copy-start.1) | copy-done | bytes 131096
  27.5 0.0 copy-start.2
  27.5 0.9 %copy-done.2 = bf16[256,256]{1,0:T(8,128)(2,1)S(1)} copy-done((bf16[256,256]{1,0:T(8,128)(2,1)S(1)}, bf16[256,256]{1,0:T(8,128)(2,1)}, u32[]{:S(2)}) %copy-start.2) | copy-done | bytes 131096
  28.4 22.3 %shard_map.65 = f32[3,8,32,256]{3,2,1,0:T(8,128)} custom-call(s32[2,8,256]{2,1,0:T(8,128)S(1)} %get-tuple-element.9.words_ref, f32[6024,128]{1,0:T(8,128)S(1)} %get-tuple-element.10.data_ref, bf16[256,640]{1,0:T(8,128)(2,1)S(1)} %get-tuple-element.11.whi_ref, bf16[256,640]{1,0:T(8,128)(2,1)S(1)} %get-tuple-element.12.wlo_ref, ...), custom_call_target="tpu_custom_call" | custom-call | tf_op jit(solution)/shard_map/pallas_call | solution.py:851
Async XLA Ops:
  0.7 1.0 %copy-start = (f32[3,32000]{1,0:T(4,128)S(1)}, f32[3,32000]{1,0:T(4,128)}, u32[]{:S(2)}) copy-start(f32[3,32000]{1,0:T(4,128)} %kern_hbm.1) | copy-start | bytes 1152004
  1.7 0.7 %copy-start.3 = (s32[3,256]{1,0:T(4,128)S(1)}, s32[3,256]{1,0:T(4,128)}, u32[]{:S(2)}) copy-start(s32[3,256]{1,0:T(4,128)} %cells_hbm.1) | copy-start | bytes 9220
  2.4 0.7 %copy-start.4 = (s32[256,1]{0,1:T(1,128)S(1)}, s32[256,1]{0,1:T(1,128)}, u32[]{:S(2)}) copy-start(s32[256,1]{0,1:T(1,128)} %param.8) | copy-start | bytes 3076
  26.5 0.9 %copy-start.1 = (bf16[256,256]{1,0:T(8,128)(2,1)S(1)}, bf16[256,256]{1,0:T(8,128)(2,1)}, u32[]{:S(2)}) copy-start(bf16[256,256]{1,0:T(8,128)(2,1)} %constant.5.clone.glo_hbm) | copy-start | bytes 393220
  27.5 0.9 %copy-start.2 = (bf16[256,256]{1,0:T(8,128)(2,1)S(1)}, bf16[256,256]{1,0:T(8,128)(2,1)}, u32[]{:S(2)}) copy-start(bf16[256,256]{1,0:T(8,128)(2,1)} %constant.4.clone.ghi_hbm) | copy-start | bytes 393220

commit v2 on v1

--- a/solution.py
+++ b/solution.py
@@ -429,7 +429,7 @@
 Y_TILES = 17
 WINDOW = CZ + 2 * HZ
 DEPTH = 2 * CX * WINDOW
-SUM_WAYS = 4
+SUM_WAYS = 16
 
 
 def gather_kernel(n_lat, n_rad, block, width_ref, tiles_hbm, cells_hbm, kern_hbm, data_ref, words_ref, whi_ref, wlo_ref,
@@ -763,9 +763,9 @@
     for c in range(3):
         acc = accs[c]
 
-        @pl.loop(0, 2)
+        @pl.loop(0, 2, unroll=2)
         def _(g):
-            @pl.loop(0, WINDOW // 8)
+            @pl.loop(0, WINDOW // 8, unroll=WINDOW // 8)
             def _(h):
                 for side in range(2):
                     v = []

time: 50.1 us -> 39.1 us (0.78)
  the two profiles are of different devices: /device:TPU:25 before, /device:TPU:1 now
where the time goes in v2:
time: 39.1 us; the launch traced here: 39 us
  Pallas kernels  34.1 us (87%)
  local copies, waits for them, and re-layouts  4.2 us (11%)
  between operations  0.68 us (2%)
    pallas_call x1, Pallas kernels, on_device_whole(): pl.pallas_call(functools.partial(gather_kernel, n_lat, n_rad, block), out...  26 us
    pallas_call x1, Pallas kernels, on_device_whole(): pl.pallas_call(functools.partial(grid_kernel, n_lat), out_shape=jax.Shape...  8.09 us
    unnamed x10, local copies, waits for them, and re-layouts  4.2 us

profile of v2, /device:TPU:1, one launch (start us, length us, event | category | flops | bytes accessed | tf_op | source)
XLA Modules:
  0.0 39.0 jit_solution(11950492355816165899)
XLA Ops:
  0.7 0.0 copy-start
  0.7 1.0 %copy-done = f32[3,32000]{1,0:T(4,128)S(1)} copy-done((f32[3,32000]{1,0:T(4,128)S(1)}, f32[3,32000]{1,0:T(4,128)}, u32[]{:S(2)}) %copy-start) | copy-done | bytes 384024
  1.7 0.0 copy-start.3
  1.7 0.7 %copy-done.3 = s32[3,256]{1,0:T(4,128)S(1)} copy-done((s32[3,256]{1,0:T(4,128)S(1)}, s32[3,256]{1,0:T(4,128)}, u32[]{:S(2)}) %copy-start.3) | copy-done | bytes 3096
  2.4 0.0 copy-start.4
  2.4 0.7 %copy-done.4 = s32[256,1]{0,1:T(1,128)S(1)} copy-done((s32[256,1]{0,1:T(1,128)S(1)}, s32[256,1]{0,1:T(1,128)}, u32[]{:S(2)}) %copy-start.4) | copy-done | bytes 1048
  3.1 26.0 %shard_map.64 = (f32[6024,128]{1,0:T(8,128)S(1)}, s32[2,8,256]{2,1,0:T(8,128)S(1)}, bf16[256,640]{1,0:T(8,128)(2,1)S(1)}, bf16[256,640]{1,0:T(8,128)(2,1)S(1)}) custom-call(s32[1]{0:T(128)S(6)} %copy.7.width_ref, s32[1,256]{1,0:T(1,128)S(1)} %bitcast.1, s32[3,256]{1,0:T(4,128)S(1)} %copy-done.3, f32[3,32000]{1,0:T(4,128)S(1)} %copy-done), custom_call_target="tpu_custom_call" | custom-call | tf_op jit(solution)/shard_map/pallas_call | solution.py:823
  29.0 0.0 copy-start.1
  29.1 0.9 %copy-done.1 = bf16[256,256]{1,0:T(8,128)(2,1)S(1)} copy-done((bf16[256,256]{1,0:T(8,128)(2,1)S(1)}, bf16[256,256]{1,0:T(8,128)(2,1)}, u32[]{:S(2)}) %copy-start.1) | copy-done | bytes 131096
  30.0 0.0 copy-start.2
  30.0 0.9 %copy-done.2 = bf16[256,256]{1,0:T(8,128)(2,1)S(1)} copy-done((bf16[256,256]{1,0:T(8,128)(2,1)S(1)}, bf16[256,256]{1,0:T(8,128)(2,1)}, u32[]{:S(2)}) %copy-start.2) | copy-done | bytes 131096
  30.9 8.1 %shard_map.65 = f32[3,8,32,256]{3,2,1,0:T(8,128)} custom-call(s32[2,8,256]{2,1,0:T(8,128)S(1)} %get-tuple-element.9.words_ref, f32[6024,128]{1,0:T(8,128)S(1)} %get-tuple-element.10.data_ref, bf16[256,640]{1,0:T(8,128)(2,1)S(1)} %get-tuple-element.11.whi_ref, bf16[256,640]{1,0:T(8,128)(2,1)S(1)} %get-tuple-element.12.wlo_ref, ...), custom_call_target="tpu_custom_call" | custom-call | tf_op jit(solution)/shard_map/pallas_call | solution.py:851
Async XLA Ops:
  0.7 1.0 %copy-start = (f32[3,32000]{1,0:T(4,128)S(1)}, f32[3,32000]{1,0:T(4,128)}, u32[]{:S(2)}) copy-start(f32[3,32000]{1,0:T(4,128)} %kern_hbm.1) | copy-start | bytes 1152004
  1.7 0.7 %copy-start.3 = (s32[3,256]{1,0:T(4,128)S(1)}, s32[3,256]{1,0:T(4,128)}, u32[]{:S(2)}) copy-start(s32[3,256]{1,0:T(4,128)} %cells_hbm.1) | copy-start | bytes 9220
  2.4 0.7 %copy-start.4 = (s32[256,1]{0,1:T(1,128)S(1)}, s32[256,1]{0,1:T(1,128)}, u32[]{:S(2)}) copy-start(s32[256,1]{0,1:T(1,128)} %param.8) | copy-start | bytes 3076
  29.0 0.9 %copy-start.1 = (bf16[256,256]{1,0:T(8,128)(2,1)S(1)}, bf16[256,256]{1,0:T(8,128)(2,1)}, u32[]{:S(2)}) copy-start(bf16[256,256]{1,0:T(8,128)(2,1)} %constant.5.clone.glo_hbm) | copy-start | bytes 393220
  30.0 0.9 %copy-start.2 = (bf16[256,256]{1,0:T(8,128)(2,1)S(1)}, bf16[256,256]{1,0:T(8,128)(2,1)}, u32[]{:S(2)}) copy-start(bf16[256,256]{1,0:T(8,128)(2,1)} %constant.4.clone.ghi_hbm) | copy-start | bytes 393220

commit v3 on v2

--- a/solution.py
+++ b/solution.py
@@ -460,8 +460,6 @@
     inner = half - 2 * edge
     mine = k * half
     spans = {"send": (mine + y * (edge + inner), edge), "inner": (mine + edge, inner), "take": (mine + (1 - y) * (edge + inner), edge)}
-    theirs = (1 - k) * half
-    other = {"send": (theirs + y * (edge + inner), edge), "inner": (theirs + edge, inner), "take": (theirs + (1 - y) * (edge + inner), edge)}
     parts = ("send", "inner")
 
     def piece(i, span):
@@ -473,28 +471,31 @@
             device_id=device, device_id_type=MESH)
 
     def z_move(i, j, up):
-        return move(i, spans[parts[j]], zs.at[i, 2 * j + (0 if up else 1)], zr.at[i, j], (lat + (2 if up else -2), rad))
+        return move(i, spans[parts[j]], zs.at[i, 0 if up else 1], zr.at[i, j], (lat + (2 if up else -2), rad))
 
     def x_move(i, j):
-        return move(i, spans[parts[j]], xs.at[i, j], xr.at[i, j], (across_x, rad))
+        return move(i, spans[parts[j]], xs.at[j], xr.at[i, j], (across_x, rad))
 
     def y_move(i, name):
-        return move(i, spans[name], ys.at[i], yr.at[i], (lat, across_y))
-
-    def k_move(i, j, of):
-        return move(i, of[("send", "inner", "take")[j]], bs.at[i, j], br.at[i, j], (lat, across_k))
+        return move(i, spans[name], ys, yr.at[i], (lat, across_y))
+
+    def k_move(i, j):
+        return move(i, spans[("send", "inner", "take")[j]], bs, br, (lat, across_k))
+
+    def sized(rows, send_sem, recv_sem, device):
+        return move(0, (0, rows), send_sem, recv_sem, device)
 
     def index_move(step):
         to = lax.rem(lat + step, n_lat)
         return pltpu.make_async_remote_copy(
-            src_ref=index_ref.at[lat], dst_ref=index_ref.at[lat], send_sem=is_sem.at[step], recv_sem=ir_sem.at[step],
+            src_ref=index_ref.at[lat], dst_ref=index_ref.at[lat], send_sem=is_sem, recv_sem=ir_sem,
             device_id=(to, rad), device_id_type=MESH)
 
-    def index_take(step):
-        whose = index_ref.at[lax.rem(lat + n_lat - step, n_lat)]
+    def index_all():
+        others = index_ref.at[pl.ds(0, n_lat - 1)]
         return pltpu.make_async_remote_copy(
-            src_ref=whose, dst_ref=whose, send_sem=is_sem.at[step], recv_sem=ir_sem.at[step],
-            device_id=(lax.rem(lat + step, n_lat), rad), device_id_type=MESH)
+            src_ref=others, dst_ref=others, send_sem=is_sem, recv_sem=ir_sem,
+            device_id=(across_x, rad), device_id_type=MESH)
 
     can_up, can_down = z < levels - 1, z > 0
     brought[1].wait()
@@ -573,10 +574,7 @@
     weights()
 
     def lists():
-        @pl.loop(1, n_lat)
-        def _(step):
-            index_take(step).wait_recv()
-
+        index_all().wait_recv()
         elements = index_ref.shape[2]
         shape = (n_lat, elements)
         rel = index_ref[:, 0, :] - lat
@@ -623,29 +621,58 @@
         def _():
             body(2 * zi)
 
+    def from_end(d, up):
+        return (z - d == 0) if up else (z + d == levels - 1)
+
+    def further(i, j, up):
+        @pl.when(can_up if up else can_down)
+        def _():
+            z_move(i, j, up).start()
+
     def line(d, up, j):
         def body(i):
             i = i + x
             z_move(i, j, up).wait_recv()
-
-            @pl.when(can_up if up else can_down)
-            def _():
-                z_move(i, j, up).start()
-
-            x_move(i, j).start()
+            further(i, j, up)
             if j == 0:
+                x_move(i, j).start()
                 y_move(i, "send").start()
-            k_move(i, j, spans).start()
+            else:
+                @pl.when(jnp.logical_not(from_end(d, up)))
+                def _():
+                    x_move(i, j).start()
+
+            k_move(i, j).start()
 
         when_there(d, up, body)
 
     def cross(d, up, j):
         def body(i):
             i = i + 1 - x
-            x_move(i, j).wait_recv()
             if j == 0:
+                x_move(i, j).wait_recv()
                 y_move(i, "send").start()
-            k_move(i, j, spans).start()
+            elif d == 0:
+                x_move(i, j).wait_recv()
+
+                @pl.when(z == 0)
+                def _():
+                    z_move(i, j, True).start()
+
+                @pl.when(z == levels - 1)
+                def _():
+                    z_move(i, j, False).start()
+            else:
+                @pl.when(from_end(d, up))
+                def _():
+                    z_move(i, j, up).wait_recv()
+                    further(i, j, up)
+
+                @pl.when(jnp.logical_not(from_end(d, up)))
+                def _():
+                    x_move(i, j).wait_recv()
+
+            k_move(i, j).start()
 
         when_there(d, up, body)
 
@@ -653,7 +680,7 @@
         def body(i):
             i = i + column
             y_move(i, "take").wait_recv()
-            k_move(i, 2, spans).start()
+            k_move(i, 2).start()
 
         when_there(d, up, body)
 
@@ -675,32 +702,39 @@
                 for up in ways(d - 2):
                     y_done(d - 2, up, 1 - x)
 
-    @pl.loop(1, n_lat)
-    def _(step):
-        index_move(step).wait_send()
-
-    @pl.loop(0, n_lat)
-    def _(i):
-        @pl.when(i != lat)
-        def _():
-            for j in range(3):
-                k_move(i, j, other).wait_recv()
-                k_move(i, j, spans).wait_send()
-            y_move(i, "send").wait_send()
-
-    @pl.loop(0, levels)
-    def _(zi):
-        i = 2 * zi + x
-        for j in range(2):
-            x_move(i, j).wait_send()
-
-            @pl.when(can_up & (zi <= z))
-            def _():
-                z_move(i, j, True).wait_send()
-
-            @pl.when(can_down & (zi >= z))
-            def _():
-                z_move(i, j, False).wait_send()
+    index_all().wait_send()
+    sized(levels * edge, xs.at[0], xr.at[0, 0], (across_x, rad)).wait_send()
+    at_end = (z == 0) | (z == levels - 1)
+    lines = levels - 1 if levels > 1 else 1
+
+    @pl.when(at_end)
+    def _():
+        sized(lines * inner, xs.at[1], xr.at[0, 1], (across_x, rad)).wait_send()
+
+    if levels > 2:
+        @pl.when(jnp.logical_not(at_end))
+        def _():
+            sized((levels - 2) * inner, xs.at[1], xr.at[0, 1], (across_x, rad)).wait_send()
+
+    for up in (True, False):
+        able, way = (can_up, 0) if up else (can_down, 1)
+        peer = (lat + (2 if up else -2), rad)
+
+        @pl.when(able)
+        def _():
+            @pl.loop(0, levels)
+            def _(zi):
+                @pl.when((zi <= z) if up else (zi >= z))
+                def _():
+                    sized(edge + inner, zs.at[2 * zi + x, way], zr.at[0, 0], peer).wait_send()
+
+            end = 0 if up else levels - 1
+            sized(inner, zs.at[2 * end + 1 - x, way], zr.at[0, 0], peer).wait_send()
+
+    sized((n_lat - 1) * edge, ys, yr.at[0], (lat, across_y)).wait_send()
+    everything = sized((n_lat - 1) * half, bs, br, (lat, across_k))
+    everything.wait_send()
+    everything.wait_recv()
 
 
 def grid_kernel(n_lat, words_ref, data_ref, whi_ref, wlo_ref, ghi_hbm, glo_hbm, out_hbm, acc0, acc1, acc2, field, result, words, ghi_ref, glo_ref, sem, smooth_sem, out_sem):
@@ -820,6 +854,7 @@
     vmem = pl.BlockSpec(memory_space=pltpu.VMEM)
     hbm = pl.BlockSpec(memory_space=pltpu.HBM)
     dma = pltpu.SemaphoreType.DMA
+    stay = functools.partial(pltpu.with_memory_space_constraint, memory_space=pltpu.HBM)
     data, words, whi, wlo = pl.pallas_call(
         functools.partial(gather_kernel, n_lat, n_rad, block),
         out_shape=[
@@ -836,14 +871,14 @@
             pltpu.VMEM(cells.shape, jnp.int32),
             pltpu.VMEM((n_lat, 8, elements), jnp.int32),
             pltpu.VMEM((8 * n_lat, DEPTH), jnp.float32),
-            dma((3,)), dma((n_lat,)), dma((n_lat,)),
-            dma((n_lat, 4)), dma((n_lat, 2)), dma((n_lat, 2)), dma((n_lat, 2)),
-            dma((n_lat,)), dma((n_lat,)), dma((n_lat, 3)), dma((n_lat, 3)),
+            dma((3,)), dma, dma,
+            dma((n_lat, 2)), dma((n_lat, 2)), dma((2,)), dma((n_lat, 2)),
+            dma, dma((n_lat,)), dma, dma,
         ],
         compiler_params=pltpu.CompilerParams(
             vmem_limit_bytes=VMEM_LIMIT, collective_id=0, has_side_effects=True
         ),
-    )(width_class, tiles.reshape(1, elements), cells, kernels)
+    )(width_class, *map(stay, (tiles.reshape(1, elements), cells, kernels)))
     smooth = band_matrix(NY, 2.5, HY).T.astype(np.float32)
     high = smooth.astype(jnp.bfloat16)
     low = (smooth - high.astype(np.float32)).astype(jnp.bfloat16)
@@ -865,7 +900,7 @@
             dma, dma((2,)), dma((3,)),
         ],
         compiler_params=pltpu.CompilerParams(vmem_limit_bytes=VMEM_LIMIT),
-    )(words, data, whi, wlo, jnp.asarray(high), jnp.asarray(low))
+    )(words, data, whi, wlo, stay(jnp.asarray(high)), stay(jnp.asarray(low)))
 
 
 def solution(mesh):

time: 39.1 us -> 33.8 us (0.86)
  local copies, waits for them, and re-layouts: 4.2 us -> 0 us
  Pallas kernels: 34.1 us -> 32.8 us
    unnamed x10 -> x0, local copies, waits for them, and re-layouts: 4.2 us -> none
    pallas_call x1, Pallas kernels: 8.09 us -> 7.38 us  [on_device_whole(): pl.pallas_call(functools.partial(grid_kernel, n_lat), out_shape=jax.Shape...]
    pallas_call x1, Pallas kernels: 26 us -> 25.5 us  [on_device_whole(): pl.pallas_call(functools.partial(gather_kernel, n_lat, n_rad, block), out...]
where the time goes in v3:
time: 33.8 us; the launch traced here: 33.5 us
  Pallas kernels  32.8 us (97%)
  between operations  0.66 us (2%)
    pallas_call x1, Pallas kernels, on_device_whole(): pl.pallas_call(functools.partial(gather_kernel, n_lat, n_rad, block), out...  25.5 us
    pallas_call x1, Pallas kernels, on_device_whole(): pl.pallas_call(functools.partial(grid_kernel, n_lat), out_shape=jax.Shape...  7.38 us

profile of v3, /device:TPU:1, one launch (start us, length us, event | category | flops | bytes accessed | tf_op | source)
XLA Modules:
  0.0 33.5 jit_solution(8875069340418239406)
XLA Ops:
  0.7 25.5 %shard_map.64 = (f32[6024,128]{1,0:T(8,128)S(1)}, s32[2,8,256]{2,1,0:T(8,128)S(1)}, bf16[256,640]{1,0:T(8,128)(2,1)S(1)}, bf16[256,640]{1,0:T(8,128)(2,1)S(1)}) custom-call(s32[1]{0:T(128)S(6)} %copy.7.width_ref, s32[1,256]{1,0:T(1,128)} %bitcast.1, s32[3,256]{1,0:T(4,128)} %cells_hbm.1, f32[3,32000]{1,0:T(4,128)} %kern_hbm.1), custom_call_target="tpu_custom_call" | custom-call | tf_op jit(solution)/shard_map/pallas_call | solution.py:858
  26.1 7.4 %shard_map.65 = f32[3,8,32,256]{3,2,1,0:T(8,128)} custom-call(s32[2,8,256]{2,1,0:T(8,128)S(1)} %get-tuple-element.9.words_ref, f32[6024,128]{1,0:T(8,128)S(1)} %get-tuple-element.10.data_ref, bf16[256,640]{1,0:T(8,128)(2,1)S(1)} %get-tuple-element.11.whi_ref, bf16[256,640]{1,0:T(8,128)(2,1)S(1)} %get-tuple-element.12.wlo_ref, ...), custom_call_target="tpu_custom_call" | custom-call | tf_op jit(solution)/shard_map/pallas_call | solution.py:886

commit v4 on v3

--- a/solution.py
+++ b/solution.py
@@ -430,6 +430,8 @@
 WINDOW = CZ + 2 * HZ
 DEPTH = 2 * CX * WINDOW
 SUM_WAYS = 16
+SUM_GROUP = 4
+CUTS = 2
 
 
 def gather_kernel(n_lat, n_rad, block, width_ref, tiles_hbm, cells_hbm, kern_hbm, data_ref, words_ref, whi_ref, wlo_ref,
@@ -456,34 +458,32 @@
         copy.start()
 
     half = block // 2
-    edge = half // 8 // 3 * 8 + 8
-    inner = half - 2 * edge
+    part = half // 2
     mine = k * half
-    spans = {"send": (mine + y * (edge + inner), edge), "inner": (mine + edge, inner), "take": (mine + (1 - y) * (edge + inner), edge)}
-    parts = ("send", "inner")
-
-    def piece(i, span):
-        return data_ref.at[pl.ds(pl.multiple_of(i * block + span[0], 8), span[1])]
-
-    def move(i, span, send_sem, recv_sem, device):
+    piece = part // CUTS
+    starts = [mine + (y if j < CUTS else 1 - y) * part + j % CUTS * piece for j in range(2 * CUTS)]
+
+    def move(row, count, send_sem, recv_sem, device):
+        rows = data_ref.at[pl.ds(pl.multiple_of(row, 8), count)]
         return pltpu.make_async_remote_copy(
-            src_ref=piece(i, span), dst_ref=piece(i, span), send_sem=send_sem, recv_sem=recv_sem,
+            src_ref=rows, dst_ref=rows, send_sem=send_sem, recv_sem=recv_sem,
             device_id=device, device_id_type=MESH)
 
     def z_move(i, j, up):
-        return move(i, spans[parts[j]], zs.at[i, 0 if up else 1], zr.at[i, j], (lat + (2 if up else -2), rad))
+        way = 0 if up else 1
+        return move(i * block + starts[j], piece, zs.at[i, way], zr.at[i, j], (lat + (2 if up else -2), rad))
 
     def x_move(i, j):
-        return move(i, spans[parts[j]], xs.at[j], xr.at[i, j], (across_x, rad))
-
-    def y_move(i, name):
-        return move(i, spans[name], ys, yr.at[i], (lat, across_y))
-
-    def k_move(i, j):
-        return move(i, spans[("send", "inner", "take")[j]], bs, br, (lat, across_k))
+        return move(i * block + starts[j], piece, xs.at[j // CUTS], xr.at[i, j], (across_x, rad))
+
+    def y_move(i, j):
+        return move(i * block + starts[j], piece, ys, yr.at[i, j % CUTS], (lat, across_y))
+
+    def k_move(i):
+        return move(i * block + mine, half, bs, br, (lat, across_k))
 
     def sized(rows, send_sem, recv_sem, device):
-        return move(0, (0, rows), send_sem, recv_sem, device)
+        return move(0, rows, send_sem, recv_sem, device)
 
     def index_move(step):
         to = lax.rem(lat + step, n_lat)
@@ -498,6 +498,8 @@
             device_id=(across_x, rad), device_id_type=MESH)
 
     can_up, can_down = z < levels - 1, z > 0
+    at_end = (z == 0) | (z == levels - 1)
+    long_up, long_down = z < levels - 2, z > 1
     brought[1].wait()
     brought[2].wait()
     index_ref[lat] = jnp.concatenate([tiles_ref[...], cells_ref[...], jnp.zeros((4, tiles_ref.shape[1]), jnp.int32)], axis=0)
@@ -522,20 +524,22 @@
         data_ref[pl.ds(base + groups * 24, room), :] = tail
     pl.semaphore_wait(barrier, n_lat - 1 + 2)
 
+    def own_z(j, up):
+        able = (long_up if up else long_down) if j >= CUTS else (can_up if up else can_down)
+
+        @pl.when(able)
+        def _():
+            z_move(lat, j, up).start()
+
+    for j in range(2 * CUTS):
+        own_z(j, True)
+        own_z(j, False)
+        if j < CUTS:
+            x_move(lat, j).start()
+
     @pl.loop(1, n_lat)
     def _(step):
         index_move(step).start()
-
-    for j in range(2):
-        @pl.when(can_up)
-        def _():
-            z_move(lat, j, True).start()
-
-        @pl.when(can_down)
-        def _():
-            z_move(lat, j, False).start()
-
-        x_move(lat, j).start()
 
     def weights():
         col = lax.broadcasted_iota(jnp.int32, (8, DEPTH), 1)
@@ -621,126 +625,130 @@
         def _():
             body(2 * zi)
 
-    def from_end(d, up):
-        return (z - d == 0) if up else (z + d == levels - 1)
-
-    def further(i, j, up):
-        @pl.when(can_up if up else can_down)
-        def _():
-            z_move(i, j, up).start()
-
     def line(d, up, j):
+        more = can_up if up else can_down
+
         def body(i):
             i = i + x
-            z_move(i, j, up).wait_recv()
-            further(i, j, up)
-            if j == 0:
+            if j < CUTS:
+                z_move(i, j, up).wait_recv()
+
+                @pl.when(more)
+                def _():
+                    z_move(i, j, up).start()
+
                 x_move(i, j).start()
-                y_move(i, "send").start()
+                if d == 1:
+                    @pl.when(jnp.logical_not(more))
+                    def _():
+                        y_move(i, j).start()
+            elif d > 1:
+                z_move(i, j, up).wait_recv()
+
+                @pl.when(more)
+                def _():
+                    z_move(i, j, up).start()
+
+                if d == levels - 1:
+                    x_move(i, j).start()
+                if j == 2 * CUTS - 1:
+                    k_move(i).start()
             else:
-                @pl.when(jnp.logical_not(from_end(d, up)))
+                @pl.when(more)
                 def _():
-                    x_move(i, j).start()
-
-            k_move(i, j).start()
+                    z_move(i, j, up).wait_recv()
+                    z_move(i, j, up).start()
+                    if j == 2 * CUTS - 1:
+                        k_move(i).start()
 
         when_there(d, up, body)
 
     def cross(d, up, j):
         def body(i):
             i = i + 1 - x
-            if j == 0:
+            if j < CUTS:
                 x_move(i, j).wait_recv()
-                y_move(i, "send").start()
-            elif d == 0:
+                if d < levels - 1:
+                    y_move(i, j).start()
+            elif d == levels - 1:
                 x_move(i, j).wait_recv()
-
-                @pl.when(z == 0)
-                def _():
-                    z_move(i, j, True).start()
-
-                @pl.when(z == levels - 1)
-                def _():
-                    z_move(i, j, False).start()
+                if j == 2 * CUTS - 1:
+                    k_move(i).start()
+
+        when_there(d, up, body)
+
+    def y_done(d, up, own_column):
+        def body(i):
+            i = i + (x if own_column else 1 - x)
+
+            def finish():
+                for j in range(CUTS):
+                    y_move(i, CUTS + j).wait_recv()
+                k_move(i).start()
+
+            if own_column:
+                pl.when(jnp.logical_not(can_up if up else can_down))(finish)
             else:
-                @pl.when(from_end(d, up))
-                def _():
-                    z_move(i, j, up).wait_recv()
-                    further(i, j, up)
-
-                @pl.when(jnp.logical_not(from_end(d, up)))
-                def _():
-                    x_move(i, j).wait_recv()
-
-            k_move(i, j).start()
+                finish()
 
         when_there(d, up, body)
 
-    def y_done(d, up, column):
-        def body(i):
-            i = i + column
-            y_move(i, "take").wait_recv()
-            k_move(i, 2).start()
-
-        when_there(d, up, body)
-
     ways = lambda d: (True, False) if d else (True,)
-    for d in range(1, levels + 2):
-        for j in range(2):
+    for d in range(1, levels + 1):
+        for j in range(CUTS):
             if d < levels:
                 for up in ways(d):
                     line(d, up, j)
-            if d - 1 < levels:
+            for up in ways(d - 1):
+                cross(d - 1, up, j)
+        if d < levels:
+            for j in range(CUTS, 2 * CUTS):
+                for up in ways(d):
+                    line(d, up, j)
+        if d == 3:
+            lists()
+        if d == levels:
+            for j in range(CUTS, 2 * CUTS):
                 for up in ways(d - 1):
                     cross(d - 1, up, j)
-            if j == 0 and d == 1:
-                lists()
-            if j == 0 and 1 <= d - 1 < levels:
-                for up in ways(d - 1):
-                    y_done(d - 1, up, x)
-            if j == 0 and 0 <= d - 2 < levels:
-                for up in ways(d - 2):
-                    y_done(d - 2, up, 1 - x)
+        if d == 2:
+            for up in ways(1):
+                y_done(1, up, True)
+        if 2 <= d <= levels:
+            for up in ways(d - 2):
+                y_done(d - 2, up, False)
 
     index_all().wait_send()
-    sized(levels * edge, xs.at[0], xr.at[0, 0], (across_x, rad)).wait_send()
-    at_end = (z == 0) | (z == levels - 1)
-    lines = levels - 1 if levels > 1 else 1
+    sized(levels * part, xs.at[0], xr.at[0, 0], (across_x, rad)).wait_send()
 
     @pl.when(at_end)
     def _():
-        sized(lines * inner, xs.at[1], xr.at[0, 1], (across_x, rad)).wait_send()
-
-    if levels > 2:
-        @pl.when(jnp.logical_not(at_end))
-        def _():
-            sized((levels - 2) * inner, xs.at[1], xr.at[0, 1], (across_x, rad)).wait_send()
+        sized(part, xs.at[1], xr.at[0, 1], (across_x, rad)).wait_send()
 
     for up in (True, False):
-        able, way = (can_up, 0) if up else (can_down, 1)
+        way = 0 if up else 1
         peer = (lat + (2 if up else -2), rad)
 
-        @pl.when(able)
-        def _():
-            @pl.loop(0, levels)
-            def _(zi):
-                @pl.when((zi <= z) if up else (zi >= z))
+        @pl.when(can_up if up else can_down)
+        def _():
+            for zi in range(levels):
+                passed = (zi <= z) if up else (zi >= z)
+                both = zi < levels - 2 if up else zi > 1
+
+                @pl.when(passed)
                 def _():
-                    sized(edge + inner, zs.at[2 * zi + x, way], zr.at[0, 0], peer).wait_send()
-
-            end = 0 if up else levels - 1
-            sized(inner, zs.at[2 * end + 1 - x, way], zr.at[0, 0], peer).wait_send()
-
-    sized((n_lat - 1) * edge, ys, yr.at[0], (lat, across_y)).wait_send()
+                    sized(2 * part if both else part, zs.at[2 * zi + x, way], zr.at[0, 0], peer).wait_send()
+
+    sized(levels * part, ys, yr.at[0, 0], (lat, across_y)).wait_send()
     everything = sized((n_lat - 1) * half, bs, br, (lat, across_k))
     everything.wait_send()
     everything.wait_recv()
 
 
-def grid_kernel(n_lat, words_ref, data_ref, whi_ref, wlo_ref, ghi_hbm, glo_hbm, out_hbm, acc0, acc1, acc2, field, result, words, ghi_ref, glo_ref, sem, smooth_sem, out_sem):
+def grid_kernel(n_lat, words_ref, data_ref, whi_ref, wlo_ref, ghi_hbm, glo_hbm, out_hbm, acc0, acc1, acc2, fields, result, words, todo, ghi_ref, glo_ref, sem, smooth_sem, out_sem):
     accs = (acc0, acc1, acc2)
     smooth = [pltpu.make_async_copy(ghi_hbm, ghi_ref, smooth_sem.at[0]), pltpu.make_async_copy(glo_hbm, glo_ref, smooth_sem.at[1])]
-    bring = pltpu.make_async_copy(words_ref, words, sem)
+    bring = pltpu.make_async_copy(words_ref, words.at[:, pl.ds(0, n_lat), :], sem)
     bring.start()
     for copy in smooth:
         copy.start()
@@ -759,15 +767,33 @@
     ramp = 25 * along
     elements = words.shape[2]
 
-    @pl.loop(0, n_lat)
-    def _(i):
-        count = words[0, i, elements - 1]
-
-        @pl.loop(0, lax.div(count + SUM_WAYS - 1, SUM_WAYS))
-        def _(step):
-            for u in range(SUM_WAYS):
-                p = step * SUM_WAYS + u
-                w0, w1 = words[0, i, p], words[1, i, p]
+    for u in range(SUM_GROUP):
+        words[0, n_lat, u] = 0
+        words[1, n_lat, u] = 0
+
+    def listed(i, n):
+        many = lax.div(words[0, i, elements - 1] + SUM_GROUP - 1, SUM_GROUP)
+
+        @pl.loop(0, lax.div(many + 7, 8))
+        def _(t):
+            for u in range(8):
+                todo[n + t * 8 + u] = (i << 16) + (t * 8 + u) * SUM_GROUP
+
+        return n + many
+
+    groups = lax.fori_loop(0, n_lat, listed, 0)
+    batch = SUM_WAYS // SUM_GROUP
+    for u in range(batch):
+        todo[groups + u] = n_lat << 16
+
+    @pl.loop(0, lax.div(groups + batch - 1, batch))
+    def _(step):
+        for g in range(batch):
+            first_slot = todo[step * batch + g]
+            i = lax.shift_right_logical(first_slot, 16)
+            p0 = first_slot & 0xFFFF
+            for u in range(SUM_GROUP):
+                w0, w1 = words[0, i, p0 + u], words[1, i, p0 + u]
                 row = w0 & 0xFFFF
                 off = lax.shift_right_logical(w0, 16) & 127
                 shift = lax.shift_right_logical(w0, 23)
@@ -795,7 +821,7 @@
     for copy in smooth:
         copy.wait()
     for c in range(3):
-        acc = accs[c]
+        acc, field = accs[c], fields.at[c]
 
         @pl.loop(0, 2, unroll=2)
         def _(g):
@@ -849,7 +875,7 @@
 
 def on_device_whole(n_lat, n_rad, kernels, cells, tiles, width_class):
     elements = tiles.shape[0]
-    block = -(-kernels.shape[1] // LANES * 3 // 16) * 16
+    block = -(-kernels.shape[1] // LANES * 3 // 32) * 32
     smem = pl.BlockSpec(memory_space=pltpu.SMEM)
     vmem = pl.BlockSpec(memory_space=pltpu.VMEM)
     hbm = pl.BlockSpec(memory_space=pltpu.HBM)
@@ -872,8 +898,8 @@
             pltpu.VMEM((n_lat, 8, elements), jnp.int32),
             pltpu.VMEM((8 * n_lat, DEPTH), jnp.float32),
             dma((3,)), dma, dma,
-            dma((n_lat, 2)), dma((n_lat, 2)), dma((2,)), dma((n_lat, 2)),
-            dma, dma((n_lat,)), dma, dma,
+            dma((n_lat, 2)), dma((n_lat, 2 * CUTS)), dma((2,)), dma((n_lat, 2 * CUTS)),
+            dma, dma((n_lat, CUTS)), dma, dma,
         ],
         compiler_params=pltpu.CompilerParams(
             vmem_limit_bytes=VMEM_LIMIT, collective_id=0, has_side_effects=True
@@ -892,9 +918,10 @@
             pltpu.VMEM((rows, LANES), jnp.float32),
             pltpu.VMEM((rows, LANES), jnp.float32),
             pltpu.VMEM((rows, LANES), jnp.float32),
-            pltpu.VMEM((DEPTH, NY), jnp.float32),
+            pltpu.VMEM((3, DEPTH, NY), jnp.float32),
             pltpu.VMEM((3, CX, CZ, NY), jnp.float32),
-            pltpu.SMEM((2, n_lat, elements), jnp.int32),
+            pltpu.SMEM((2, n_lat + 1, elements), jnp.int32),
+            pltpu.SMEM((n_lat * elements // SUM_GROUP + 16,), jnp.int32),
             pltpu.VMEM((NY, NY), jnp.bfloat16),
             pltpu.VMEM((NY, NY), jnp.bfloat16),
             dma, dma((2,)), dma((3,)),
@@ -905,7 +932,7 @@
 
 def solution(mesh):
     n_lat, n_rad = mesh.shape["lat"], mesh.shape["rad"]
-    whole = n_lat <= 8 and n_lat % 2 == 0 and n_rad == 4
+    whole = n_lat == 8 and n_rad == 4
     return jax.shard_map(
         functools.partial(on_device_whole if whole else on_device, n_lat, n_rad),
         mesh=mesh,

time: 33.8 us -> 32.6 us (0.964)
  the two profiles are of different devices: /device:TPU:1 before, /device:TPU:25 now
where the time goes in v4:
time: 32.6 us; the launch traced here: 32.2 us
  Pallas kernels  31.5 us (97%)
  between operations  0.66 us (2%)
    pallas_call x1, Pallas kernels, on_device_whole(): pl.pallas_call(functools.partial(gather_kernel, n_lat, n_rad, block), out...  22.5 us
    pallas_call x1, Pallas kernels, on_device_whole(): pl.pallas_call(functools.partial(grid_kernel, n_lat), out_shape=jax.Shape...  9.08 us

profile of v4, /device:TPU:25, one launch (start us, length us, event | category | flops | bytes accessed | tf_op | source)
XLA Modules:
  0.0 32.2 jit_solution(622084595935780492)
XLA Ops:
  0.7 22.5 %shard_map.64 = (f32[6152,128]{1,0:T(8,128)S(1)}, s32[2,8,256]{2,1,0:T(8,128)S(1)}, bf16[256,640]{1,0:T(8,128)(2,1)S(1)}, bf16[256,640]{1,0:T(8,128)(2,1)S(1)}) custom-call(s32[1]{0:T(128)S(6)} %copy.7.width_ref, s32[1,256]{1,0:T(1,128)} %bitcast.1, s32[3,256]{1,0:T(4,128)} %cells_hbm.1, f32[3,32000]{1,0:T(4,128)} %kern_hbm.1), custom_call_target="tpu_custom_call" | custom-call | tf_op jit(solution)/shard_map/pallas_call | solution.py:884
  23.1 9.1 %shard_map.65 = f32[3,8,32,256]{3,2,1,0:T(8,128)} custom-call(s32[2,8,256]{2,1,0:T(8,128)S(1)} %get-tuple-element.9.words_ref, f32[6152,128]{1,0:T(8,128)S(1)} %get-tuple-element.10.data_ref, bf16[256,640]{1,0:T(8,128)(2,1)S(1)} %get-tuple-element.11.whi_ref, bf16[256,640]{1,0:T(8,128)(2,1)S(1)} %get-tuple-element.12.wlo_ref, ...), custom_call_target="tpu_custom_call" | custom-call | tf_op jit(solution)/shard_map/pallas_call | solution.py:912

commit v5 on v4

--- a/solution.py
+++ b/solution.py
@@ -431,7 +431,7 @@
 DEPTH = 2 * CX * WINDOW
 SUM_WAYS = 16
 SUM_GROUP = 4
-CUTS = 2
+CUTS = 3
 
 
 def gather_kernel(n_lat, n_rad, block, width_ref, tiles_hbm, cells_hbm, kern_hbm, data_ref, words_ref, whi_ref, wlo_ref,
@@ -531,11 +531,16 @@
         def _():
             z_move(lat, j, up).start()
 
-    for j in range(2 * CUTS):
+    for j in range(CUTS):
         own_z(j, True)
         own_z(j, False)
-        if j < CUTS:
-            x_move(lat, j).start()
+        x_move(lat, j).start()
+    for j in range(CUTS, 2 * CUTS):
+        for up in (True, False):
+            if j == CUTS:
+                own_z(j, up)
+            else:
+                pl.when(z == (0 if up else levels - 1))(functools.partial(own_z, j, up))
 
     @pl.loop(1, n_lat)
     def _(step):
@@ -616,7 +621,7 @@
         words_ref[0] = jnp.where(lane == elements - 1, total, words)
         zb = jnp.maximum(lax.shift_right_logical(zq, 2) - 1, 0)
         at = ((beside * Z_BINS + zb) * Y_TILES + lax.shift_right_logical(y0, 4)) * 8
-        words_ref[1] = at | ((zq & 7) << 16) | ((y0 & 15) << 20) | (code << 24)
+        words_ref[1] = at | ((zq & 7) << 12) | ((y0 & 127) << 16) | (code << 24)
 
     def when_there(d, up, body):
         zi = z - d if up else z + d
@@ -624,6 +629,19 @@
         @pl.when((zi >= 0) & (zi < levels))
         def _():
             body(2 * zi)
+
+    def later_own():
+        for j in range(CUTS + 1, 2 * CUTS):
+            for up in (True, False):
+                pl.when(z != (0 if up else levels - 1))(functools.partial(own_z, j, up))
+
+    def extra(d, up, farthest):
+        end = (z == d) if up else (z == levels - 1 - d)
+
+        @pl.when(end if farthest else jnp.logical_not(end))
+        def _():
+            for j in range(CUTS, 2 * CUTS):
+                line(d, up, j)
 
     def line(d, up, j):
         more = can_up if up else can_down
@@ -701,11 +719,17 @@
                     line(d, up, j)
             for up in ways(d - 1):
                 cross(d - 1, up, j)
+            if d == 3 and j == 0:
+                for up in ways(1):
+                    extra(1, up, False)
         if d < levels:
-            for j in range(CUTS, 2 * CUTS):
-                for up in ways(d):
-                    line(d, up, j)
+            for up in ways(d):
+                extra(d, up, True)
+        if d == 1:
+            later_own()
         if d == 3:
+            for up in ways(2):
+                extra(2, up, False)
             lists()
         if d == levels:
             for j in range(CUTS, 2 * CUTS):
@@ -764,7 +788,6 @@
     sub = lax.broadcasted_iota(jnp.int32, (8, LANES), 0)
     across = lane & 15
     along = lax.shift_right_logical(lane, 4)
-    ramp = 25 * along
     elements = words.shape[2]
 
     for u in range(SUM_GROUP):
@@ -797,17 +820,19 @@
                 row = w0 & 0xFFFF
                 off = lax.shift_right_logical(w0, 16) & 127
                 shift = lax.shift_right_logical(w0, 23)
-                at = pl.multiple_of(w1 & 0xFFFF, 8)
-                zq = lax.shift_right_logical(w1, 16) & 7
-                yl = lax.shift_right_logical(w1, 20) & 15
+                at = pl.multiple_of(w1 & 0xFFF, 8)
+                zq = lax.shift_right_logical(w1, 12) & 7
+                y0 = lax.shift_right_logical(w1, 16) & 127
                 low = lax.shift_right_logical(w1, 24) & 7
                 wide = lax.shift_right_logical(w1, 27)
                 tz = (sub - zq) & 7
-                ty = (lane - yl) & 15
-                tx = along - low
-                index = (ramp + shift + 5 * tz + ty) & (LANES - 1)
+                turned = (lane - y0) & (LANES - 1)
+                ty = turned & 15
+                xl = lax.shift_right_logical(turned, 4)
+                tx = xl - low
+                index = (25 * xl + shift + 5 * tz + ty) & (LANES - 1)
                 good = (tz < 5) & (ty < 5) & (tx >= 0) & (tx < wide)
-                first = across >= yl
+                first = across >= (y0 & 15)
                 here, there = good & first, good & jnp.logical_not(first)
                 head = lane >= off
                 for c in range(3):
@@ -835,21 +860,9 @@
                             return acc[pl.ds(pl.multiple_of(r, 8), 8), :]
 
                         v.append(bins(1) + jnp.where(low_half, bins(0), bins(2)))
-                    for bit in (4, 2, 1):
-                        straight = (along & bit) == 0
-                        w = list(v)
-                        for r in range(8):
-                            if r & bit:
-                                continue
-                            a, b = v[r], v[r + bit]
-                            if bit == 4:
-                                turned = pltpu.roll(jnp.where(straight, b, a), 64, 1)
-                                w[r] = jnp.where(straight, a, turned)
-                                w[r + bit] = jnp.where(straight, turned, b)
-                            else:
-                                w[r] = jnp.where(straight, a, pltpu.roll(b, 16 * bit, 1))
-                                w[r + bit] = jnp.where(straight, pltpu.roll(a, LANES - 16 * bit, 1), b)
-                        v = w
+                    for bit in (1, 2, 4):
+                        v = [jnp.where((along & bit) == 0, v[t], v[(t + bit) % 8]) for t in range(8)]
+                    v = [v[0]] + [pltpu.roll(v[8 - xl], LANES - 16 * xl, 1) for xl in range(1, 8)]
                     for xl in range(8):
                         r = pl.multiple_of(g * (CX * WINDOW) + xl * WINDOW + h * 8, 8)
                         field[pl.ds(r, 8), side * LANES : (side + 1) * LANES] = v[xl]

time: 32.6 us -> 31.7 us (0.972)
  the two profiles are of different devices: /device:TPU:25 before, /device:TPU:1 now
where the time goes in v5:
time: 31.7 us; the launch traced here: 31.4 us
  Pallas kernels  30.8 us (97%)
  between operations  0.66 us (2%)
    pallas_call x1, Pallas kernels, on_device_whole(): pl.pallas_call(functools.partial(gather_kernel, n_lat, n_rad, block), out...  24.6 us
    pallas_call x1, Pallas kernels, on_device_whole(): pl.pallas_call(functools.partial(grid_kernel, n_lat), out_shape=jax.Shape...  6.2 us

profile of v5, /device:TPU:1, one launch (start us, length us, event | category | flops | bytes accessed | tf_op | source)
XLA Modules:
  0.0 31.4 jit_solution(6123324362752688050)
XLA Ops:
  0.7 24.6 %shard_map.64 = (f32[6152,128]{1,0:T(8,128)S(1)}, s32[2,8,256]{2,1,0:T(8,128)S(1)}, bf16[256,640]{1,0:T(8,128)(2,1)S(1)}, bf16[256,640]{1,0:T(8,128)(2,1)S(1)}) custom-call(s32[1]{0:T(128)S(6)} %copy.7.width_ref, s32[1,256]{1,0:T(1,128)} %bitcast.1, s32[3,256]{1,0:T(4,128)} %cells_hbm.1, f32[3,32000]{1,0:T(4,128)} %kern_hbm.1), custom_call_target="tpu_custom_call" | custom-call | tf_op jit(solution)/shard_map/pallas_call | solution.py:897
  25.2 6.2 %shard_map.65 = f32[3,8,32,256]{3,2,1,0:T(8,128)} custom-call(s32[2,8,256]{2,1,0:T(8,128)S(1)} %get-tuple-element.9.words_ref, f32[6152,128]{1,0:T(8,128)S(1)} %get-tuple-element.10.data_ref, bf16[256,640]{1,0:T(8,128)(2,1)S(1)} %get-tuple-element.11.whi_ref, bf16[256,640]{1,0:T(8,128)(2,1)S(1)} %get-tuple-element.12.wlo_ref, ...), custom_call_target="tpu_custom_call" | custom-call | tf_op jit(solution)/shard_map/pallas_call | solution.py:925

commit v6 on v5

--- a/solution.py
+++ b/solution.py
@@ -429,7 +429,7 @@
 Y_TILES = 17
 WINDOW = CZ + 2 * HZ
 DEPTH = 2 * CX * WINDOW
-SUM_WAYS = 16
+SUM_WAYS = 24
 SUM_GROUP = 4
 CUTS = 3
 
@@ -449,13 +449,18 @@
 
     for peer in (across_y, across_k):
         pl.semaphore_signal(barrier, inc=1, device_id=(lat, peer), device_id_type=MESH)
+    points = kern_hbm.shape[1]
+    split = block // 6 * LANES
     brought = [
-        pltpu.make_async_copy(kern_hbm, kern_ref, in_sem.at[0]),
+        pltpu.make_async_copy(kern_hbm.at[:, :split], kern_ref.at[:, :split], in_sem.at[0]),
+        pltpu.make_async_copy(kern_hbm.at[:, split:], kern_ref.at[:, split:points], in_sem.at[3]),
         pltpu.make_async_copy(tiles_hbm, tiles_ref, in_sem.at[1]),
         pltpu.make_async_copy(cells_hbm, cells_ref, in_sem.at[2]),
     ]
     for copy in brought:
         copy.start()
+    if kern_ref.shape[1] > points:
+        kern_ref[:, points:] = jnp.zeros((3, kern_ref.shape[1] - points), jnp.float32)
 
     half = block // 2
     part = half // 2
@@ -500,28 +505,28 @@
     can_up, can_down = z < levels - 1, z > 0
     at_end = (z == 0) | (z == levels - 1)
     long_up, long_down = z < levels - 2, z > 1
-    brought[1].wait()
-    brought[2].wait()
-    index_ref[lat] = jnp.concatenate([tiles_ref[...], cells_ref[...], jnp.zeros((4, tiles_ref.shape[1]), jnp.int32)], axis=0)
-    brought[0].wait()
     base = pl.multiple_of(lat * block, 8)
-    lane_tiles = kern_ref.shape[1] // LANES
-    groups = lane_tiles // 8
-
-    def packed(at, row, count):
-        rows = [kern_ref[:, pl.ds(pl.multiple_of(at + u * LANES, LANES), LANES)] for u in range(count)]
-        return jnp.concatenate(rows, axis=0)
-
-    @pl.loop(0, groups, unroll=4)
-    def _(g):
-        data_ref[pl.ds(base + pl.multiple_of(g * 24, 8), 24), :] = packed(g * 8 * LANES, 0, 8)
-
-    left = lane_tiles - groups * 8
-    if left:
-        tail = packed(groups * 8 * LANES, 0, left)
-        room = block - groups * 24
-        tail = jnp.concatenate([tail, jnp.zeros((room - 3 * left, LANES), jnp.float32)], axis=0)
-        data_ref[pl.ds(base + groups * 24, room), :] = tail
+    sets = block // 24
+
+    def pack(first, count):
+        @pl.loop(0, count, unroll=4)
+        def _(g):
+            at = (first + g) * 8 * LANES
+            rows = [kern_ref[:, pl.ds(pl.multiple_of(at + u * LANES, LANES), LANES)] for u in range(8)]
+            data_ref[pl.ds(base + pl.multiple_of((first + g) * 24, 8), 24), :] = jnp.concatenate(rows, axis=0)
+
+    def pack_part(j):
+        pack(k * (sets // 2) + (y if j == 0 else 1 - y) * (sets // 4), sets // 4)
+
+    @pl.when(k == 0)
+    def _():
+        brought[0].wait()
+
+    @pl.when(k == 1)
+    def _():
+        brought[1].wait()
+
+    pack_part(0)
     pl.semaphore_wait(barrier, n_lat - 1 + 2)
 
     def own_z(j, up):
@@ -535,6 +540,7 @@
         own_z(j, True)
         own_z(j, False)
         x_move(lat, j).start()
+    pack_part(1)
     for j in range(CUTS, 2 * CUTS):
         for up in (True, False):
             if j == CUTS:
@@ -542,9 +548,23 @@
             else:
                 pl.when(z == (0 if up else levels - 1))(functools.partial(own_z, j, up))
 
+    brought[2].wait()
+    brought[3].wait()
+    index_ref[lat] = jnp.concatenate([tiles_ref[...], cells_ref[...], jnp.zeros((4, tiles_ref.shape[1]), jnp.int32)], axis=0)
+
     @pl.loop(1, n_lat)
     def _(step):
         index_move(step).start()
+
+    @pl.when(k == 1)
+    def _():
+        brought[0].wait()
+
+    @pl.when(k == 0)
+    def _():
+        brought[1].wait()
+
+    pack((1 - k) * (sets // 2), sets // 2)
 
     def weights():
         col = lax.broadcasted_iota(jnp.int32, (8, DEPTH), 1)
@@ -818,27 +838,29 @@
             for u in range(SUM_GROUP):
                 w0, w1 = words[0, i, p0 + u], words[1, i, p0 + u]
                 row = w0 & 0xFFFF
-                off = lax.shift_right_logical(w0, 16) & 127
-                shift = lax.shift_right_logical(w0, 23)
                 at = pl.multiple_of(w1 & 0xFFF, 8)
-                zq = lax.shift_right_logical(w1, 12) & 7
-                y0 = lax.shift_right_logical(w1, 16) & 127
-                low = lax.shift_right_logical(w1, 24) & 7
-                wide = lax.shift_right_logical(w1, 27)
+                v0, v1 = jnp.full((8, LANES), w0, jnp.int32), jnp.full((8, LANES), w1, jnp.int32)
+                off = lax.shift_right_logical(v0, 16) & 127
+                shift = lax.shift_right_logical(v0, 23)
+                zq = lax.shift_right_logical(v1, 12)
+                y0 = lax.shift_right_logical(v1, 16)
+                low = lax.shift_right_logical(v1, 24)
+                wide = lax.shift_right_logical(v1, 27)
                 tz = (sub - zq) & 7
                 turned = (lane - y0) & (LANES - 1)
                 ty = turned & 15
                 xl = lax.shift_right_logical(turned, 4)
-                tx = xl - low
+                tx = (xl - low) & 7
                 index = (25 * xl + shift + 5 * tz + ty) & (LANES - 1)
-                good = (tz < 5) & (ty < 5) & (tx >= 0) & (tx < wide)
+                good = (jnp.maximum(tz, ty) < 5) & (tx < wide)
                 first = across >= (y0 & 15)
                 here, there = good & first, good & jnp.logical_not(first)
                 head = lane >= off
                 for c in range(3):
-                    a = jnp.broadcast_to(data_ref[pl.ds(row + c, 1), :], (8, LANES))
-                    b = jnp.broadcast_to(data_ref[pl.ds(row + 3 + c, 1), :], (8, LANES))
-                    v = jnp.take_along_axis(jnp.where(head, a, b), index, axis=1, mode="promise_in_bounds")
+                    a = data_ref[pl.ds(row + c, 1), :]
+                    b = data_ref[pl.ds(row + 3 + c, 1), :]
+                    v = jnp.broadcast_to(jnp.where(head[0:1], a, b), (8, LANES))
+                    v = jnp.take_along_axis(v, index, axis=1, mode="promise_in_bounds")
                     accs[c][pl.ds(at, 8), :] += jnp.where(here, v, 0.0)
                     accs[c][pl.ds(at + 8, 8), :] += jnp.where(there, v, 0.0)
 
@@ -888,7 +910,7 @@
 
 def on_device_whole(n_lat, n_rad, kernels, cells, tiles, width_class):
     elements = tiles.shape[0]
-    block = -(-kernels.shape[1] // LANES * 3 // 32) * 32
+    block = -(-kernels.shape[1] // LANES * 3 // 96) * 96
     smem = pl.BlockSpec(memory_space=pltpu.SMEM)
     vmem = pl.BlockSpec(memory_space=pltpu.VMEM)
     hbm = pl.BlockSpec(memory_space=pltpu.HBM)
@@ -905,12 +927,12 @@
         in_specs=[smem, hbm, hbm, hbm],
         out_specs=[vmem] * 4,
         scratch_shapes=[
-            pltpu.VMEM(kernels.shape, jnp.float32),
+            pltpu.VMEM((3, block // 3 * LANES), jnp.float32),
             pltpu.VMEM((1, elements), jnp.int32),
             pltpu.VMEM(cells.shape, jnp.int32),
             pltpu.VMEM((n_lat, 8, elements), jnp.int32),
             pltpu.VMEM((8 * n_lat, DEPTH), jnp.float32),
-            dma((3,)), dma, dma,
+            dma((4,)), dma, dma,
             dma((n_lat, 2)), dma((n_lat, 2 * CUTS)), dma((2,)), dma((n_lat, 2 * CUTS)),
             dma, dma((n_lat, CUTS)), dma, dma,
         ],

time: 31.7 us -> 31.5 us (level); the launches traced: 31.4 us -> 31.6 us
  no operation moved by 1% of the time
where the time goes in v6:
time: 31.5 us; the launch traced here: 31.6 us
  Pallas kernels  31 us (98%)
  between operations  0.66 us (2%)
    pallas_call x1, Pallas kernels, on_device_whole(): pl.pallas_call(functools.partial(gather_kernel, n_lat, n_rad, block), out...  24.6 us
    pallas_call x1, Pallas kernels, on_device_whole(): pl.pallas_call(functools.partial(grid_kernel, n_lat), out_shape=jax.Shape...  6.4 us

profile of v6, /device:TPU:1, one launch (start us, length us, event | category | flops | bytes accessed | tf_op | source)
XLA Modules:
  0.0 31.6 jit_solution(17155216926948604559)
XLA Ops:
  0.7 24.6 %shard_map.64 = (f32[6152,128]{1,0:T(8,128)S(1)}, s32[2,8,256]{2,1,0:T(8,128)S(1)}, bf16[256,640]{1,0:T(8,128)(2,1)S(1)}, bf16[256,640]{1,0:T(8,128)(2,1)S(1)}) custom-call(s32[1]{0:T(128)S(6)} %copy.7.width_ref, s32[1,256]{1,0:T(1,128)} %bitcast.1, s32[3,256]{1,0:T(4,128)} %cells_hbm.1, f32[3,32000]{1,0:T(4,128)} %kern_hbm.1), custom_call_target="tpu_custom_call" | custom-call | tf_op jit(solution)/shard_map/pallas_call | solution.py:919
  25.2 6.4 %shard_map.65 = f32[3,8,32,256]{3,2,1,0:T(8,128)} custom-call(s32[2,8,256]{2,1,0:T(8,128)S(1)} %get-tuple-element.9.words_ref, f32[6152,128]{1,0:T(8,128)S(1)} %get-tuple-element.10.data_ref, bf16[256,640]{1,0:T(8,128)(2,1)S(1)} %get-tuple-element.11.whi_ref, bf16[256,640]{1,0:T(8,128)(2,1)S(1)} %get-tuple-element.12.wlo_ref, ...), custom_call_target="tpu_custom_call" | custom-call | tf_op jit(solution)/shard_map/pallas_call | solution.py:947

commit v7 on v6

--- a/solution.py
+++ b/solution.py
@@ -429,7 +429,7 @@
 Y_TILES = 17
 WINDOW = CZ + 2 * HZ
 DEPTH = 2 * CX * WINDOW
-SUM_WAYS = 24
+SUM_WAYS = 32
 SUM_GROUP = 4
 CUTS = 3
 

time: 31.5 us -> 32.5 us (1.032)
  Pallas kernels: 31 us -> 32 us
    pallas_call x1, Pallas kernels: 6.4 us -> 7.47 us  [on_device_whole(): pl.pallas_call(functools.partial(grid_kernel, n_lat), out_shape=jax.Shape...]
where the time goes in v7:
time: 32.5 us; the launch traced here: 32.7 us
  Pallas kernels  32 us (98%)
  between operations  0.66 us (2%)
    pallas_call x1, Pallas kernels, on_device_whole(): pl.pallas_call(functools.partial(gather_kernel, n_lat, n_rad, block), out...  24.6 us
    pallas_call x1, Pallas kernels, on_device_whole(): pl.pallas_call(functools.partial(grid_kernel, n_lat), out_shape=jax.Shape...  7.47 us

profile of v7, /device:TPU:1, one launch (start us, length us, event | category | flops | bytes accessed | tf_op | source)
XLA Modules:
  0.0 32.7 jit_solution(1621537562959059948)
XLA Ops:
  0.7 24.6 %shard_map.64 = (f32[6152,128]{1,0:T(8,128)S(1)}, s32[2,8,256]{2,1,0:T(8,128)S(1)}, bf16[256,640]{1,0:T(8,128)(2,1)S(1)}, bf16[256,640]{1,0:T(8,128)(2,1)S(1)}) custom-call(s32[1]{0:T(128)S(6)} %copy.7.width_ref, s32[1,256]{1,0:T(1,128)} %bitcast.1, s32[3,256]{1,0:T(4,128)} %cells_hbm.1, f32[3,32000]{1,0:T(4,128)} %kern_hbm.1), custom_call_target="tpu_custom_call" | custom-call | tf_op jit(solution)/shard_map/pallas_call | solution.py:919
  25.2 7.5 %shard_map.65 = f32[3,8,32,256]{3,2,1,0:T(8,128)} custom-call(s32[2,8,256]{2,1,0:T(8,128)S(1)} %get-tuple-element.9.words_ref, f32[6152,128]{1,0:T(8,128)S(1)} %get-tuple-element.10.data_ref, bf16[256,640]{1,0:T(8,128)(2,1)S(1)} %get-tuple-element.11.whi_ref, bf16[256,640]{1,0:T(8,128)(2,1)S(1)} %get-tuple-element.12.wlo_ref, ...), custom_call_target="tpu_custom_call" | custom-call | tf_op jit(solution)/shard_map/pallas_call | solution.py:947
